TPU v7x, 128 devices: a whole 4x4x4 slice. The times are simulated.
128 devices in a mesh: dp: 4 (over x), depth: 32 (over z, y, core).
Axes of the slice: x: 4, y: 4, z: 4, core: 2. Of those that a mesh axis runs over, the one named last changes fastest.
Arguments:
- c_states: float32 [32, 1024, 1024], P('depth', 'dp'), parts along dimension 1, may hold values from -20 to 20
- w_query: bfloat16 [64, 1024, 1024], P('depth'), may hold values from -16 to 16
- w_key: bfloat16 [64, 1024, 1024], P('depth'), may hold values from -8 to 8
- w_value: bfloat16 [64, 1024, 1024], P('depth'), may hold values from -0.1875 to 0.1875
- w_out: bfloat16 [64, 1024, 1024], P('depth'), may hold values from -0.1875 to 0.1875
Outputs:
- states: float32 [64, 1024, 1024], P('depth', 'dp'), parts along dimension 1
- residual_rms: float32 [4], P('dp'), parts along dimension 0
There are 4 independent parts, one for each index of `dp`. A program takes and returns all parts, laid end to end along the dimension named above; an argument that names none is the same for every part. Nothing has to cross between parts.
All inputs are finite; a program needn't handle non-finite values.
Results may differ from a plain program's by a relative error of at most 0.006.
Values sent between devices are 32-bit elements; how exact they have to be, the bound alone decides.
No kernel may reach another device: no remote copies, remote signals or barrier semaphores. Data moves between devices by JAX's collectives and lax.ppermute only.
A program may use at most 384 MiB of HBM per device.

v0:
```python
import jax
import jax.numpy as jnp
from jax import lax
from jax.sharding import PartitionSpec as P

HEADS = 8
HEAD_DIM = 128
INNER = 1024


def from_behind(block, axis, distance):
    devices = range(lax.axis_size(axis))
    route = [(i - distance, i) for i in devices if i - distance in devices]
    return lax.ppermute(block, axis, route)


def normalize_rows(state):
    row_mean = jnp.mean(state, axis=-1, keepdims=True)
    centred = state - row_mean
    row_var = jnp.mean(centred * centred, axis=-1, keepdims=True)
    return centred * lax.rsqrt(row_var + 1e-05)


def apply_layer(state, w_query, w_key, w_value, w_out):
    tokens = state.shape[0]
    normed = normalize_rows(state).astype(jnp.bfloat16)
    query_rows = jnp.dot(normed, w_query, preferred_element_type=jnp.float32).astype(jnp.bfloat16)
    key_rows = jnp.dot(normed, w_key, preferred_element_type=jnp.float32).astype(jnp.bfloat16)
    value_rows = jnp.dot(normed, w_value, preferred_element_type=jnp.float32).astype(jnp.bfloat16)
    query_heads = query_rows.reshape(tokens, HEADS, HEAD_DIM)
    key_heads = key_rows.reshape(tokens, HEADS, HEAD_DIM)
    value_heads = value_rows.reshape(tokens, HEADS, HEAD_DIM)
    scores = jnp.einsum(
        "qhd,khd->hqk", query_heads, key_heads, preferred_element_type=jnp.float32
    ) * HEAD_DIM ** (-0.5)
    attn_probs = jax.nn.softmax(scores, axis=-1).astype(jnp.bfloat16)
    context = jnp.einsum(
        "hqk,khd->qhd", attn_probs, value_heads, preferred_element_type=jnp.float32
    )
    context = context.reshape(tokens, INNER).astype(jnp.bfloat16)
    return state + jnp.dot(context, w_out, preferred_element_type=jnp.float32)


def exact_dot(left, right):
    return jnp.dot(left, right, precision=lax.Precision.HIGHEST)


def per_device(c_states, w_query, w_key, w_value, w_out):
    c_guess = c_states[0]
    dev_index = lax.axis_index("depth")
    dev_count = lax.axis_size("depth")
    tokens = c_guess.shape[0]
    width = c_guess.shape[1]
    fine_f = apply_layer(c_guess, w_query[0], w_key[0], w_value[0], w_out[0])
    fine_c = apply_layer(fine_f, w_query[1], w_key[1], w_value[1], w_out[1])
    next_state = from_behind(c_guess, "depth", -1)
    residual = fine_c - next_state
    counted = dev_index < dev_count - 1
    part_sq = jnp.where(counted, jnp.sum(residual * residual), jnp.zeros((), jnp.float32))
    total_sq = lax.psum(part_sq, "depth")
    residual_rms = jnp.sqrt(total_sq / ((dev_count - 1) * tokens * width)).reshape(1)
    identity_m = jnp.eye(width, dtype=jnp.float32)
    coarse_map = identity_m + 0.25 * jnp.dot(
        w_value[1], w_out[1], preferred_element_type=jnp.float32
    )
    zero_rows = jnp.zeros((tokens, width), jnp.float32)

    def advance(position, state_tuple):
        correction, carried, candidate = state_tuple
        received = from_behind(candidate, "depth", 1)
        is_next = dev_index == position + 1
        correction = jnp.where(is_next, received, correction)
        carried = lax.cond(
            is_next,
            lambda arriving: exact_dot(arriving, coarse_map),
            lambda arriving: carried,
            received,
        )
        candidate = jnp.where(is_next, carried + residual, candidate)
        return (correction, carried, candidate)

    correction, carried, unused_last = lax.fori_loop(
        0, dev_count - 1, advance, (zero_rows, zero_rows, residual)
    )
    new_state = fine_c + carried
    relaxed = apply_layer(c_guess + correction, w_query[0], w_key[0], w_value[0], w_out[0])
    return (jnp.stack([relaxed, new_state]), residual_rms)


def solution(mesh):
    in_specs = (
        P("depth", "dp", None),
        P("depth", None, None),
        P("depth", None, None),
        P("depth", None, None),
        P("depth", None, None),
    )
    out_specs = (P("depth", "dp", None), P("dp"))
    return jax.shard_map(
        per_device, mesh=mesh, in_specs=in_specs, out_specs=out_specs, check_vma=False
    )
```

profile of v0, /device:TPU:121, one launch (start us, length us, event | category | flops | bytes accessed | tf_op | source)
XLA Modules:
  0.0 792.7 jit_solution(12508386384208237097)
XLA Ops:
  30.7 5.9 multiply_add_fusion
  37.5 3.5 multiply_reduce_fusion.3
  42.1 659.8 %while.21 = (s32[]{:T(128)}, f32[256,1024]{1,0:T(8,128)}, f32[256,1024]{1,0:T(8,128)S(1)}, f32[256,1024]{1,0:T(8,128)}, s32[]{:T(128)}, /*index=5*/f32[1024,1024...) while((s32[]{:T(128)}, f32[256,1024]{1,0:T(8,128)}, f32[256,1024]{1,0:T(8,128)S(1)}, ...), condition=%wide.region_11.12_spmd.clone, body=%wide.region_8.11_spmd.clone.sunk | while | flops 3222274048 | bytes 17825972 | solution.py:82
  51.6 14.6 %collective-permute-done = f32[256,1024]{1,0:T(8,128)S(1)} collective-permute-done((f32[256,1024]{1,0:T(8,128)}, f32[256,1024]{1,0:T(8,128)S(1)}, u32[]{:S(2)}, u32[]{:S(2)}) %collective-permute-start) | collective-permute-done | bytes 1048608 | tf_op jit(solution)/shard_map/while/body/eval_jaxpr/ppermute | solution.py:14
  66.2 3.5 select_select_fusion.2
  71.0 15.0 %collective-permute-done = f32[256,1024]{1,0:T(8,128)S(1)} collective-permute-done((f32[256,1024]{1,0:T(8,128)}, f32[256,1024]{1,0:T(8,128)S(1)}, u32[]{:S(2)}, u32[]{:S(2)}) %collective-permute-start) | collective-permute-done | bytes 1048608 | tf_op jit(solution)/shard_map/while/body/eval_jaxpr/ppermute | solution.py:14
  86.0 3.5 select_select_fusion.2
  90.8 15.0 %collective-permute-done = f32[256,1024]{1,0:T(8,128)S(1)} collective-permute-done((f32[256,1024]{1,0:T(8,128)}, f32[256,1024]{1,0:T(8,128)S(1)}, u32[]{:S(2)}, u32[]{:S(2)}) %collective-permute-start) | collective-permute-done | bytes 1048608 | tf_op jit(solution)/shard_map/while/body/eval_jaxpr/ppermute | solution.py:14
  105.8 3.5 select_select_fusion.2
  110.6 15.0 %collective-permute-done = f32[256,1024]{1,0:T(8,128)S(1)} collective-permute-done((f32[256,1024]{1,0:T(8,128)}, f32[256,1024]{1,0:T(8,128)S(1)}, u32[]{:S(2)}, u32[]{:S(2)}) %collective-permute-start) | collective-permute-done | bytes 1048608 | tf_op jit(solution)/shard_map/while/body/eval_jaxpr/ppermute | solution.py:14
  125.7 3.5 select_select_fusion.2
  130.5 15.0 %collective-permute-done = f32[256,1024]{1,0:T(8,128)S(1)} collective-permute-done((f32[256,1024]{1,0:T(8,128)}, f32[256,1024]{1,0:T(8,128)S(1)}, u32[]{:S(2)}, u32[]{:S(2)}) %collective-permute-start) | collective-permute-done | bytes 1048608 | tf_op jit(solution)/shard_map/while/body/eval_jaxpr/ppermute | solution.py:14
  145.5 3.5 select_select_fusion.2
  150.3 15.0 %collective-permute-done = f32[256,1024]{1,0:T(8,128)S(1)} collective-permute-done((f32[256,1024]{1,0:T(8,128)}, f32[256,1024]{1,0:T(8,128)S(1)}, u32[]{:S(2)}, u32[]{:S(2)}) %collective-permute-start) | collective-permute-done | bytes 1048608 | tf_op jit(solution)/shard_map/while/body/eval_jaxpr/ppermute | solution.py:14
  165.3 3.5 select_select_fusion.2
  170.1 15.0 %collective-permute-done = f32[256,1024]{1,0:T(8,128)S(1)} collective-permute-done((f32[256,1024]{1,0:T(8,128)}, f32[256,1024]{1,0:T(8,128)S(1)}, u32[]{:S(2)}, u32[]{:S(2)}) %collective-permute-start) | collective-permute-done | bytes 1048608 | tf_op jit(solution)/shard_map/while/body/eval_jaxpr/ppermute | solution.py:14
  185.1 3.5 select_select_fusion.2
  189.9 15.0 %collective-permute-done = f32[256,1024]{1,0:T(8,128)S(1)} collective-permute-done((f32[256,1024]{1,0:T(8,128)}, f32[256,1024]{1,0:T(8,128)S(1)}, u32[]{:S(2)}, u32[]{:S(2)}) %collective-permute-start) | collective-permute-done | bytes 1048608 | tf_op jit(solution)/shard_map/while/body/eval_jaxpr/ppermute | solution.py:14
  204.9 3.5 select_select_fusion.2
  209.7 15.0 %collective-permute-done = f32[256,1024]{1,0:T(8,128)S(1)} collective-permute-done((f32[256,1024]{1,0:T(8,128)}, f32[256,1024]{1,0:T(8,128)S(1)}, u32[]{:S(2)}, u32[]{:S(2)}) %collective-permute-start) | collective-permute-done | bytes 1048608 | tf_op jit(solution)/shard_map/while/body/eval_jaxpr/ppermute | solution.py:14
  224.7 3.5 select_select_fusion.2
  229.5 15.0 %collective-permute-done = f32[256,1024]{1,0:T(8,128)S(1)} collective-permute-done((f32[256,1024]{1,0:T(8,128)}, f32[256,1024]{1,0:T(8,128)S(1)}, u32[]{:S(2)}, u32[]{:S(2)}) %collective-permute-start) | collective-permute-done | bytes 1048608 | tf_op jit(solution)/shard_map/while/body/eval_jaxpr/ppermute | solution.py:14
  244.6 3.5 select_select_fusion.2
  249.4 15.0 %collective-permute-done = f32[256,1024]{1,0:T(8,128)S(1)} collective-permute-done((f32[256,1024]{1,0:T(8,128)}, f32[256,1024]{1,0:T(8,128)S(1)}, u32[]{:S(2)}, u32[]{:S(2)}) %collective-permute-start) | collective-permute-done | bytes 1048608 | tf_op jit(solution)/shard_map/while/body/eval_jaxpr/ppermute | solution.py:14
  264.4 3.5 select_select_fusion.2
  269.2 15.0 %collective-permute-done = f32[256,1024]{1,0:T(8,128)S(1)} collective-permute-done((f32[256,1024]{1,0:T(8,128)}, f32[256,1024]{1,0:T(8,128)S(1)}, u32[]{:S(2)}, u32[]{:S(2)}) %collective-permute-start) | collective-permute-done | bytes 1048608 | tf_op jit(solution)/shard_map/while/body/eval_jaxpr/ppermute | solution.py:14
  284.2 3.5 select_select_fusion.2
  289.0 15.0 %collective-permute-done = f32[256,1024]{1,0:T(8,128)S(1)} collective-permute-done((f32[256,1024]{1,0:T(8,128)}, f32[256,1024]{1,0:T(8,128)S(1)}, u32[]{:S(2)}, u32[]{:S(2)}) %collective-permute-start) | collective-permute-done | bytes 1048608 | tf_op jit(solution)/shard_map/while/body/eval_jaxpr/ppermute | solution.py:14
  304.0 3.5 select_select_fusion.2
  308.8 15.0 %collective-permute-done = f32[256,1024]{1,0:T(8,128)S(1)} collective-permute-done((f32[256,1024]{1,0:T(8,128)}, f32[256,1024]{1,0:T(8,128)S(1)}, u32[]{:S(2)}, u32[]{:S(2)}) %collective-permute-start) | collective-permute-done | bytes 1048608 | tf_op jit(solution)/shard_map/while/body/eval_jaxpr/ppermute | solution.py:14
  323.8 3.5 select_select_fusion.2
  328.6 15.0 %collective-permute-done = f32[256,1024]{1,0:T(8,128)S(1)} collective-permute-done((f32[256,1024]{1,0:T(8,128)}, f32[256,1024]{1,0:T(8,128)S(1)}, u32[]{:S(2)}, u32[]{:S(2)}) %collective-permute-start) | collective-permute-done | bytes 1048608 | tf_op jit(solution)/shard_map/while/body/eval_jaxpr/ppermute | solution.py:14
  343.6 3.5 select_select_fusion.2
  348.4 15.0 %collective-permute-done = f32[256,1024]{1,0:T(8,128)S(1)} collective-permute-done((f32[256,1024]{1,0:T(8,128)}, f32[256,1024]{1,0:T(8,128)S(1)}, u32[]{:S(2)}, u32[]{:S(2)}) %collective-permute-start) | collective-permute-done | bytes 1048608 | tf_op jit(solution)/shard_map/while/body/eval_jaxpr/ppermute | solution.py:14
  363.5 3.5 select_select_fusion.2
  368.3 15.0 %collective-permute-done = f32[256,1024]{1,0:T(8,128)S(1)} collective-permute-done((f32[256,1024]{1,0:T(8,128)}, f32[256,1024]{1,0:T(8,128)S(1)}, u32[]{:S(2)}, u32[]{:S(2)}) %collective-permute-start) | collective-permute-done | bytes 1048608 | tf_op jit(solution)/shard_map/while/body/eval_jaxpr/ppermute | solution.py:14
  383.3 3.5 select_select_fusion.2
  388.1 15.0 %collective-permute-done = f32[256,1024]{1,0:T(8,128)S(1)} collective-permute-done((f32[256,1024]{1,0:T(8,128)}, f32[256,1024]{1,0:T(8,128)S(1)}, u32[]{:S(2)}, u32[]{:S(2)}) %collective-permute-start) | collective-permute-done | bytes 1048608 | tf_op jit(solution)/shard_map/while/body/eval_jaxpr/ppermute | solution.py:14
  403.1 3.5 select_select_fusion.2
  407.9 15.0 %collective-permute-done = f32[256,1024]{1,0:T(8,128)S(1)} collective-permute-done((f32[256,1024]{1,0:T(8,128)}, f32[256,1024]{1,0:T(8,128)S(1)}, u32[]{:S(2)}, u32[]{:S(2)}) %collective-permute-start) | collective-permute-done | bytes 1048608 | tf_op jit(solution)/shard_map/while/body/eval_jaxpr/ppermute | solution.py:14
  422.9 3.5 select_select_fusion.2
  427.7 15.0 %collective-permute-done = f32[256,1024]{1,0:T(8,128)S(1)} collective-permute-done((f32[256,1024]{1,0:T(8,128)}, f32[256,1024]{1,0:T(8,128)S(1)}, u32[]{:S(2)}, u32[]{:S(2)}) %collective-permute-start) | collective-permute-done | bytes 1048608 | tf_op jit(solution)/shard_map/while/body/eval_jaxpr/ppermute | solution.py:14
  442.7 3.5 select_select_fusion.2
  447.5 15.0 %collective-permute-done = f32[256,1024]{1,0:T(8,128)S(1)} collective-permute-done((f32[256,1024]{1,0:T(8,128)}, f32[256,1024]{1,0:T(8,128)S(1)}, u32[]{:S(2)}, u32[]{:S(2)}) %collective-permute-start) | collective-permute-done | bytes 1048608 | tf_op jit(solution)/shard_map/while/body/eval_jaxpr/ppermute | solution.py:14
  462.5 3.5 select_select_fusion.2
  467.3 15.0 %collective-permute-done = f32[256,1024]{1,0:T(8,128)S(1)} collective-permute-done((f32[256,1024]{1,0:T(8,128)}, f32[256,1024]{1,0:T(8,128)S(1)}, u32[]{:S(2)}, u32[]{:S(2)}) %collective-permute-start) | collective-permute-done | bytes 1048608 | tf_op jit(solution)/shard_map/while/body/eval_jaxpr/ppermute | solution.py:14
  482.4 3.5 select_select_fusion.2
  487.2 15.0 %collective-permute-done = f32[256,1024]{1,0:T(8,128)S(1)} collective-permute-done((f32[256,1024]{1,0:T(8,128)}, f32[256,1024]{1,0:T(8,128)S(1)}, u32[]{:S(2)}, u32[]{:S(2)}) %collective-permute-start) | collective-permute-done | bytes 1048608 | tf_op jit(solution)/shard_map/while/body/eval_jaxpr/ppermute | solution.py:14
  502.2 3.5 select_select_fusion.2
  507.0 15.7 %collective-permute-done = f32[256,1024]{1,0:T(8,128)S(1)} collective-permute-done((f32[256,1024]{1,0:T(8,128)}, f32[256,1024]{1,0:T(8,128)S(1)}, u32[]{:S(2)}, u32[]{:S(2)}) %collective-permute-start) | collective-permute-done | bytes 1048608 | tf_op jit(solution)/shard_map/while/body/eval_jaxpr/ppermute | solution.py:14
  522.7 3.5 select_select_fusion.2
  527.5 17.1 %collective-permute-done = f32[256,1024]{1,0:T(8,128)S(1)} collective-permute-done((f32[256,1024]{1,0:T(8,128)}, f32[256,1024]{1,0:T(8,128)S(1)}, u32[]{:S(2)}, u32[]{:S(2)}) %collective-permute-start) | collective-permute-done | bytes 1048608 | tf_op jit(solution)/shard_map/while/body/eval_jaxpr/ppermute | solution.py:14
  544.6 3.5 select_select_fusion.2
  549.4 17.1 %collective-permute-done = f32[256,1024]{1,0:T(8,128)S(1)} collective-permute-done((f32[256,1024]{1,0:T(8,128)}, f32[256,1024]{1,0:T(8,128)S(1)}, u32[]{:S(2)}, u32[]{:S(2)}) %collective-permute-start) | collective-permute-done | bytes 1048608 | tf_op jit(solution)/shard_map/while/body/eval_jaxpr/ppermute | solution.py:14
  566.5 3.5 select_select_fusion.2
  571.3 17.1 %collective-permute-done = f32[256,1024]{1,0:T(8,128)S(1)} collective-permute-done((f32[256,1024]{1,0:T(8,128)}, f32[256,1024]{1,0:T(8,128)S(1)}, u32[]{:S(2)}, u32[]{:S(2)}) %collective-permute-start) | collective-permute-done | bytes 1048608 | tf_op jit(solution)/shard_map/while/body/eval_jaxpr/ppermute | solution.py:14
  588.5 3.5 select_select_fusion.2
  593.3 17.1 %collective-permute-done = f32[256,1024]{1,0:T(8,128)S(1)} collective-permute-done((f32[256,1024]{1,0:T(8,128)}, f32[256,1024]{1,0:T(8,128)S(1)}, u32[]{:S(2)}, u32[]{:S(2)}) %collective-permute-start) | collective-permute-done | bytes 1048608 | tf_op jit(solution)/shard_map/while/body/eval_jaxpr/ppermute | solution.py:14
  610.4 3.5 select_select_fusion.2
  615.2 17.1 %collective-permute-done = f32[256,1024]{1,0:T(8,128)S(1)} collective-permute-done((f32[256,1024]{1,0:T(8,128)}, f32[256,1024]{1,0:T(8,128)S(1)}, u32[]{:S(2)}, u32[]{:S(2)}) %collective-permute-start) | collective-permute-done | bytes 1048608 | tf_op jit(solution)/shard_map/while/body/eval_jaxpr/ppermute | solution.py:14
  637.1 55.9 %collective-permute-done = f32[256,1024]{1,0:T(8,128)S(1)} collective-permute-done((f32[256,1024]{1,0:T(8,128)}, f32[256,1024]{1,0:T(8,128)S(1)}, u32[]{:S(2)}, u32[]{:S(2)}) %collective-permute-start) | collective-permute-done | bytes 1048608 | tf_op jit(solution)/shard_map/while/body/eval_jaxpr/ppermute | solution.py:14
  693.1 5.7 conditional.3
  693.1 5.7 fusion.178
  711.0 70.6 %psum.7 = f32[]{:T(128)} all-reduce(f32[]{:T(128)S(6)} %select_n.28), channel_id=1, replica_groups=mesh['dp'=4,'depth'=32] {'depth'}, use_global_device_ids=true, to_apply=%region_17.18 | all-reduce | flops 1 | bytes 8 | tf_op jit(solution)/shard_map/psum | solution.py:60
  (132 shorter events, 102.6 us)
Async XLA Ops:
  0.6 5.7 copy-start
  0.6 35.9 %collective-permute-start.1 = (f32[256,1024]{1,0:T(8,128)}, f32[256,1024]{1,0:T(8,128)S(1)}, u32[]{:S(2)}, u32[]{:S(2)}) collective-permute-start(f32[256,1024]{1,0:T(8,128)} %bitcast.197), channel_id=1, source_target_pairs={{1,0},{2,1},{3,2},{4,3},{5,4},{6,5},{7,6},{8,7},{9,8},{10,9},{11,1... | collective-permute-start | bytes 3145736 | tf_op jit(solution)/shard_map/ppermute | solution.py:14
  6.3 3.5 copy-start.11
  6.5 4.8 copy-start.8
  15.5 2.8 copy-start.1
  18.4 2.2 copy-start.6
  19.5 2.6 copy-start.12
  20.5 3.0 copy-start.9
  27.8 2.8 copy-start.2
  36.5 1.0 copy-start.5
  42.3 4.8 collective-permute-start
  50.3 15.9 %collective-permute-start = (f32[256,1024]{1,0:T(8,128)}, f32[256,1024]{1,0:T(8,128)S(1)}, u32[]{:S(2)}, u32[]{:S(2)}) collective-permute-start(f32[256,1024]{1,0:T(8,128)} %get-tuple-element.255), channel_id=1, source_target_pairs={{0,1},{1,2},{2,3},{3,4},{4,5},{5,6},{6,7},{7,8},{8,9},{9,10},{10,1... | collective-permute-start | bytes 3145736 | tf_op jit(solution)/shard_map/while/body/eval_jaxpr/ppermute | solution.py:14
  69.7 16.3 %collective-permute-start = (f32[256,1024]{1,0:T(8,128)}, f32[256,1024]{1,0:T(8,128)S(1)}, u32[]{:S(2)}, u32[]{:S(2)}) collective-permute-start(f32[256,1024]{1,0:T(8,128)} %get-tuple-element.255), channel_id=1, source_target_pairs={{0,1},{1,2},{2,3},{3,4},{4,5},{5,6},{6,7},{7,8},{8,9},{9,10},{10,1... | collective-permute-start | bytes 3145736 | tf_op jit(solution)/shard_map/while/body/eval_jaxpr/ppermute | solution.py:14
  89.5 16.3 %collective-permute-start = (f32[256,1024]{1,0:T(8,128)}, f32[256,1024]{1,0:T(8,128)S(1)}, u32[]{:S(2)}, u32[]{:S(2)}) collective-permute-start(f32[256,1024]{1,0:T(8,128)} %get-tuple-element.255), channel_id=1, source_target_pairs={{0,1},{1,2},{2,3},{3,4},{4,5},{5,6},{6,7},{7,8},{8,9},{9,10},{10,1... | collective-permute-start | bytes 3145736 | tf_op jit(solution)/shard_map/while/body/eval_jaxpr/ppermute | solution.py:14
  109.3 16.3 %collective-permute-start = (f32[256,1024]{1,0:T(8,128)}, f32[256,1024]{1,0:T(8,128)S(1)}, u32[]{:S(2)}, u32[]{:S(2)}) collective-permute-start(f32[256,1024]{1,0:T(8,128)} %get-tuple-element.255), channel_id=1, source_target_pairs={{0,1},{1,2},{2,3},{3,4},{4,5},{5,6},{6,7},{7,8},{8,9},{9,10},{10,1... | collective-permute-start | bytes 3145736 | tf_op jit(solution)/shard_map/while/body/eval_jaxpr/ppermute | solution.py:14
  129.2 16.3 %collective-permute-start = (f32[256,1024]{1,0:T(8,128)}, f32[256,1024]{1,0:T(8,128)S(1)}, u32[]{:S(2)}, u32[]{:S(2)}) collective-permute-start(f32[256,1024]{1,0:T(8,128)} %get-tuple-element.255), channel_id=1, source_target_pairs={{0,1},{1,2},{2,3},{3,4},{4,5},{5,6},{6,7},{7,8},{8,9},{9,10},{10,1... | collective-permute-start | bytes 3145736 | tf_op jit(solution)/shard_map/while/body/eval_jaxpr/ppermute | solution.py:14
  149.0 16.3 %collective-permute-start = (f32[256,1024]{1,0:T(8,128)}, f32[256,1024]{1,0:T(8,128)S(1)}, u32[]{:S(2)}, u32[]{:S(2)}) collective-permute-start(f32[256,1024]{1,0:T(8,128)} %get-tuple-element.255), channel_id=1, source_target_pairs={{0,1},{1,2},{2,3},{3,4},{4,5},{5,6},{6,7},{7,8},{8,9},{9,10},{10,1... | collective-permute-start | bytes 3145736 | tf_op jit(solution)/shard_map/while/body/eval_jaxpr/ppermute | solution.py:14
  168.8 16.3 %collective-permute-start = (f32[256,1024]{1,0:T(8,128)}, f32[256,1024]{1,0:T(8,128)S(1)}, u32[]{:S(2)}, u32[]{:S(2)}) collective-permute-start(f32[256,1024]{1,0:T(8,128)} %get-tuple-element.255), channel_id=1, source_target_pairs={{0,1},{1,2},{2,3},{3,4},{4,5},{5,6},{6,7},{7,8},{8,9},{9,10},{10,1... | collective-permute-start | bytes 3145736 | tf_op jit(solution)/shard_map/while/body/eval_jaxpr/ppermute | solution.py:14
  188.6 16.3 %collective-permute-start = (f32[256,1024]{1,0:T(8,128)}, f32[256,1024]{1,0:T(8,128)S(1)}, u32[]{:S(2)}, u32[]{:S(2)}) collective-permute-start(f32[256,1024]{1,0:T(8,128)} %get-tuple-element.255), channel_id=1, source_target_pairs={{0,1},{1,2},{2,3},{3,4},{4,5},{5,6},{6,7},{7,8},{8,9},{9,10},{10,1... | collective-permute-start | bytes 3145736 | tf_op jit(solution)/shard_map/while/body/eval_jaxpr/ppermute | solution.py:14
  208.4 16.3 %collective-permute-start = (f32[256,1024]{1,0:T(8,128)}, f32[256,1024]{1,0:T(8,128)S(1)}, u32[]{:S(2)}, u32[]{:S(2)}) collective-permute-start(f32[256,1024]{1,0:T(8,128)} %get-tuple-element.255), channel_id=1, source_target_pairs={{0,1},{1,2},{2,3},{3,4},{4,5},{5,6},{6,7},{7,8},{8,9},{9,10},{10,1... | collective-permute-start | bytes 3145736 | tf_op jit(solution)/shard_map/while/body/eval_jaxpr/ppermute | solution.py:14
  228.2 16.3 %collective-permute-start = (f32[256,1024]{1,0:T(8,128)}, f32[256,1024]{1,0:T(8,128)S(1)}, u32[]{:S(2)}, u32[]{:S(2)}) collective-permute-start(f32[256,1024]{1,0:T(8,128)} %get-tuple-element.255), channel_id=1, source_target_pairs={{0,1},{1,2},{2,3},{3,4},{4,5},{5,6},{6,7},{7,8},{8,9},{9,10},{10,1... | collective-permute-start | bytes 3145736 | tf_op jit(solution)/shard_map/while/body/eval_jaxpr/ppermute | solution.py:14
  248.1 16.3 %collective-permute-start = (f32[256,1024]{1,0:T(8,128)}, f32[256,1024]{1,0:T(8,128)S(1)}, u32[]{:S(2)}, u32[]{:S(2)}) collective-permute-start(f32[256,1024]{1,0:T(8,128)} %get-tuple-element.255), channel_id=1, source_target_pairs={{0,1},{1,2},{2,3},{3,4},{4,5},{5,6},{6,7},{7,8},{8,9},{9,10},{10,1... | collective-permute-start | bytes 3145736 | tf_op jit(solution)/shard_map/while/body/eval_jaxpr/ppermute | solution.py:14
  267.9 16.3 %collective-permute-start = (f32[256,1024]{1,0:T(8,128)}, f32[256,1024]{1,0:T(8,128)S(1)}, u32[]{:S(2)}, u32[]{:S(2)}) collective-permute-start(f32[256,1024]{1,0:T(8,128)} %get-tuple-element.255), channel_id=1, source_target_pairs={{0,1},{1,2},{2,3},{3,4},{4,5},{5,6},{6,7},{7,8},{8,9},{9,10},{10,1... | collective-permute-start | bytes 3145736 | tf_op jit(solution)/shard_map/while/body/eval_jaxpr/ppermute | solution.py:14
  287.7 16.3 %collective-permute-start = (f32[256,1024]{1,0:T(8,128)}, f32[256,1024]{1,0:T(8,128)S(1)}, u32[]{:S(2)}, u32[]{:S(2)}) collective-permute-start(f32[256,1024]{1,0:T(8,128)} %get-tuple-element.255), channel_id=1, source_target_pairs={{0,1},{1,2},{2,3},{3,4},{4,5},{5,6},{6,7},{7,8},{8,9},{9,10},{10,1... | collective-permute-start | bytes 3145736 | tf_op jit(solution)/shard_map/while/body/eval_jaxpr/ppermute | solution.py:14
  307.5 16.3 %collective-permute-start = (f32[256,1024]{1,0:T(8,128)}, f32[256,1024]{1,0:T(8,128)S(1)}, u32[]{:S(2)}, u32[]{:S(2)}) collective-permute-start(f32[256,1024]{1,0:T(8,128)} %get-tuple-element.255), channel_id=1, source_target_pairs={{0,1},{1,2},{2,3},{3,4},{4,5},{5,6},{6,7},{7,8},{8,9},{9,10},{10,1... | collective-permute-start | bytes 3145736 | tf_op jit(solution)/shard_map/while/body/eval_jaxpr/ppermute | solution.py:14
  327.3 16.3 %collective-permute-start = (f32[256,1024]{1,0:T(8,128)}, f32[256,1024]{1,0:T(8,128)S(1)}, u32[]{:S(2)}, u32[]{:S(2)}) collective-permute-start(f32[256,1024]{1,0:T(8,128)} %get-tuple-element.255), channel_id=1, source_target_pairs={{0,1},{1,2},{2,3},{3,4},{4,5},{5,6},{6,7},{7,8},{8,9},{9,10},{10,1... | collective-permute-start | bytes 3145736 | tf_op jit(solution)/shard_map/while/body/eval_jaxpr/ppermute | solution.py:14
  347.1 16.3 %collective-permute-start = (f32[256,1024]{1,0:T(8,128)}, f32[256,1024]{1,0:T(8,128)S(1)}, u32[]{:S(2)}, u32[]{:S(2)}) collective-permute-start(f32[256,1024]{1,0:T(8,128)} %get-tuple-element.255), channel_id=1, source_target_pairs={{0,1},{1,2},{2,3},{3,4},{4,5},{5,6},{6,7},{7,8},{8,9},{9,10},{10,1... | collective-permute-start | bytes 3145736 | tf_op jit(solution)/shard_map/while/body/eval_jaxpr/ppermute | solution.py:14
  367.0 16.3 %collective-permute-start = (f32[256,1024]{1,0:T(8,128)}, f32[256,1024]{1,0:T(8,128)S(1)}, u32[]{:S(2)}, u32[]{:S(2)}) collective-permute-start(f32[256,1024]{1,0:T(8,128)} %get-tuple-element.255), channel_id=1, source_target_pairs={{0,1},{1,2},{2,3},{3,4},{4,5},{5,6},{6,7},{7,8},{8,9},{9,10},{10,1... | collective-permute-start | bytes 3145736 | tf_op jit(solution)/shard_map/while/body/eval_jaxpr/ppermute | solution.py:14
  386.8 16.3 %collective-permute-start = (f32[256,1024]{1,0:T(8,128)}, f32[256,1024]{1,0:T(8,128)S(1)}, u32[]{:S(2)}, u32[]{:S(2)}) collective-permute-start(f32[256,1024]{1,0:T(8,128)} %get-tuple-element.255), channel_id=1, source_target_pairs={{0,1},{1,2},{2,3},{3,4},{4,5},{5,6},{6,7},{7,8},{8,9},{9,10},{10,1... | collective-permute-start | bytes 3145736 | tf_op jit(solution)/shard_map/while/body/eval_jaxpr/ppermute | solution.py:14
  406.6 16.3 %collective-permute-start = (f32[256,1024]{1,0:T(8,128)}, f32[256,1024]{1,0:T(8,128)S(1)}, u32[]{:S(2)}, u32[]{:S(2)}) collective-permute-start(f32[256,1024]{1,0:T(8,128)} %get-tuple-element.255), channel_id=1, source_target_pairs={{0,1},{1,2},{2,3},{3,4},{4,5},{5,6},{6,7},{7,8},{8,9},{9,10},{10,1... | collective-permute-start | bytes 3145736 | tf_op jit(solution)/shard_map/while/body/eval_jaxpr/ppermute | solution.py:14
  426.4 16.3 %collective-permute-start = (f32[256,1024]{1,0:T(8,128)}, f32[256,1024]{1,0:T(8,128)S(1)}, u32[]{:S(2)}, u32[]{:S(2)}) collective-permute-start(f32[256,1024]{1,0:T(8,128)} %get-tuple-element.255), channel_id=1, source_target_pairs={{0,1},{1,2},{2,3},{3,4},{4,5},{5,6},{6,7},{7,8},{8,9},{9,10},{10,1... | collective-permute-start | bytes 3145736 | tf_op jit(solution)/shard_map/while/body/eval_jaxpr/ppermute | solution.py:14
  446.2 16.3 %collective-permute-start = (f32[256,1024]{1,0:T(8,128)}, f32[256,1024]{1,0:T(8,128)S(1)}, u32[]{:S(2)}, u32[]{:S(2)}) collective-permute-start(f32[256,1024]{1,0:T(8,128)} %get-tuple-element.255), channel_id=1, source_target_pairs={{0,1},{1,2},{2,3},{3,4},{4,5},{5,6},{6,7},{7,8},{8,9},{9,10},{10,1... | collective-permute-start | bytes 3145736 | tf_op jit(solution)/shard_map/while/body/eval_jaxpr/ppermute | solution.py:14
  466.0 16.3 %collective-permute-start = (f32[256,1024]{1,0:T(8,128)}, f32[256,1024]{1,0:T(8,128)S(1)}, u32[]{:S(2)}, u32[]{:S(2)}) collective-permute-start(f32[256,1024]{1,0:T(8,128)} %get-tuple-element.255), channel_id=1, source_target_pairs={{0,1},{1,2},{2,3},{3,4},{4,5},{5,6},{6,7},{7,8},{8,9},{9,10},{10,1... | collective-permute-start | bytes 3145736 | tf_op jit(solution)/shard_map/while/body/eval_jaxpr/ppermute | solution.py:14
  485.9 16.3 %collective-permute-start = (f32[256,1024]{1,0:T(8,128)}, f32[256,1024]{1,0:T(8,128)S(1)}, u32[]{:S(2)}, u32[]{:S(2)}) collective-permute-start(f32[256,1024]{1,0:T(8,128)} %get-tuple-element.255), channel_id=1, source_target_pairs={{0,1},{1,2},{2,3},{3,4},{4,5},{5,6},{6,7},{7,8},{8,9},{9,10},{10,1... | collective-permute-start | bytes 3145736 | tf_op jit(solution)/shard_map/while/body/eval_jaxpr/ppermute | solution.py:14
  505.7 17.0 %collective-permute-start = (f32[256,1024]{1,0:T(8,128)}, f32[256,1024]{1,0:T(8,128)S(1)}, u32[]{:S(2)}, u32[]{:S(2)}) collective-permute-start(f32[256,1024]{1,0:T(8,128)} %get-tuple-element.255), channel_id=1, source_target_pairs={{0,1},{1,2},{2,3},{3,4},{4,5},{5,6},{6,7},{7,8},{8,9},{9,10},{10,1... | collective-permute-start | bytes 3145736 | tf_op jit(solution)/shard_map/while/body/eval_jaxpr/ppermute | solution.py:14
  526.2 18.4 %collective-permute-start = (f32[256,1024]{1,0:T(8,128)}, f32[256,1024]{1,0:T(8,128)S(1)}, u32[]{:S(2)}, u32[]{:S(2)}) collective-permute-start(f32[256,1024]{1,0:T(8,128)} %get-tuple-element.255), channel_id=1, source_target_pairs={{0,1},{1,2},{2,3},{3,4},{4,5},{5,6},{6,7},{7,8},{8,9},{9,10},{10,1... | collective-permute-start | bytes 3145736 | tf_op jit(solution)/shard_map/while/body/eval_jaxpr/ppermute | solution.py:14
  548.1 18.4 %collective-permute-start = (f32[256,1024]{1,0:T(8,128)}, f32[256,1024]{1,0:T(8,128)S(1)}, u32[]{:S(2)}, u32[]{:S(2)}) collective-permute-start(f32[256,1024]{1,0:T(8,128)} %get-tuple-element.255), channel_id=1, source_target_pairs={{0,1},{1,2},{2,3},{3,4},{4,5},{5,6},{6,7},{7,8},{8,9},{9,10},{10,1... | collective-permute-start | bytes 3145736 | tf_op jit(solution)/shard_map/while/body/eval_jaxpr/ppermute | solution.py:14
  570.0 18.4 %collective-permute-start = (f32[256,1024]{1,0:T(8,128)}, f32[256,1024]{1,0:T(8,128)S(1)}, u32[]{:S(2)}, u32[]{:S(2)}) collective-permute-start(f32[256,1024]{1,0:T(8,128)} %get-tuple-element.255), channel_id=1, source_target_pairs={{0,1},{1,2},{2,3},{3,4},{4,5},{5,6},{6,7},{7,8},{8,9},{9,10},{10,1... | collective-permute-start | bytes 3145736 | tf_op jit(solution)/shard_map/while/body/eval_jaxpr/ppermute | solution.py:14
  592.0 18.4 %collective-permute-start = (f32[256,1024]{1,0:T(8,128)}, f32[256,1024]{1,0:T(8,128)S(1)}, u32[]{:S(2)}, u32[]{:S(2)}) collective-permute-start(f32[256,1024]{1,0:T(8,128)} %get-tuple-element.255), channel_id=1, source_target_pairs={{0,1},{1,2},{2,3},{3,4},{4,5},{5,6},{6,7},{7,8},{8,9},{9,10},{10,1... | collective-permute-start | bytes 3145736 | tf_op jit(solution)/shard_map/while/body/eval_jaxpr/ppermute | solution.py:14
  613.9 18.4 %collective-permute-start = (f32[256,1024]{1,0:T(8,128)}, f32[256,1024]{1,0:T(8,128)S(1)}, u32[]{:S(2)}, u32[]{:S(2)}) collective-permute-start(f32[256,1024]{1,0:T(8,128)} %get-tuple-element.255), channel_id=1, source_target_pairs={{0,1},{1,2},{2,3},{3,4},{4,5},{5,6},{6,7},{7,8},{8,9},{9,10},{10,1... | collective-permute-start | bytes 3145736 | tf_op jit(solution)/shard_map/while/body/eval_jaxpr/ppermute | solution.py:14
  635.8 57.2 %collective-permute-start = (f32[256,1024]{1,0:T(8,128)}, f32[256,1024]{1,0:T(8,128)S(1)}, u32[]{:S(2)}, u32[]{:S(2)}) collective-permute-start(f32[256,1024]{1,0:T(8,128)} %get-tuple-element.255), channel_id=1, source_target_pairs={{0,1},{1,2},{2,3},{3,4},{4,5},{5,6},{6,7},{7,8},{8,9},{9,10},{10,1... | collective-permute-start | bytes 3145736 | tf_op jit(solution)/shard_map/while/body/eval_jaxpr/ppermute | solution.py:14
  702.0 2.8 copy-start.7
  704.1 2.4 copy-start.10
  785.7 2.8 copy-start.3
  788.6 1.2 copy-start.4
where the time goes:
time: 806 us; the launch traced here: 793 us
  waiting for transfers between devices  506 us (63%)
  other arithmetic  115 us (14%)
  blocking collectives  70.6 us (9%)
  matrix products  47.3 us (6%)
  starting transfers between devices  42.5 us (5%)
    ppermute x32, waiting for transfers between devices, from_behind(): return lax.ppermute(block, axis, route)  506 us
    select_n x31, other arithmetic, advance(): correction = jnp.where(is_next, received, correction)  108 us
    psum x1, blocking collectives, per_device(): total_sq = lax.psum(part_sq, 'depth')  70.6 us
    ppermute x32, starting transfers between devices, from_behind(): return lax.ppermute(block, axis, route)  42.5 us
  transfers between devices with their start and end apart: 32, of which 31 were waited for; matrix products, arithmetic and copies ran while one was open for 4% of the time, Pallas kernels for 0%

commit v1 on v0

v1 whole, which is shorter than its diff:
```python
import functools

import jax
import jax.numpy as jnp
from jax import lax
from jax.experimental import pallas as pl
from jax.experimental.pallas import tpu as pltpu
from jax.sharding import PartitionSpec as P

HEADS = 8
HEAD_DIM = 128
INNER = 1024
CHUNKS = 4

BF = jnp.bfloat16
F32 = jnp.float32
IN_VMEM = pl.BlockSpec(memory_space=pltpu.VMEM)
IN_SMEM = pl.BlockSpec(memory_space=pltpu.SMEM)


def normalize_rows(state):
    row_mean = jnp.mean(state, axis=-1, keepdims=True)
    centred = state - row_mean
    row_var = jnp.mean(centred * centred, axis=-1, keepdims=True)
    return centred * lax.rsqrt(row_var + 1e-05)


def apply_layer(state, w_query, w_key, w_value, w_out):
    tokens = state.shape[0]
    normed = normalize_rows(state).astype(jnp.bfloat16)
    query_rows = jnp.dot(normed, w_query, preferred_element_type=jnp.float32).astype(jnp.bfloat16)
    key_rows = jnp.dot(normed, w_key, preferred_element_type=jnp.float32).astype(jnp.bfloat16)
    value_rows = jnp.dot(normed, w_value, preferred_element_type=jnp.float32).astype(jnp.bfloat16)
    query_heads = query_rows.reshape(tokens, HEADS, HEAD_DIM)
    key_heads = key_rows.reshape(tokens, HEADS, HEAD_DIM)
    value_heads = value_rows.reshape(tokens, HEADS, HEAD_DIM)
    scores = jnp.einsum(
        "qhd,khd->hqk", query_heads, key_heads, preferred_element_type=jnp.float32
    ) * HEAD_DIM ** (-0.5)
    attn_probs = jax.nn.softmax(scores, axis=-1).astype(jnp.bfloat16)
    context = jnp.einsum(
        "hqk,khd->qhd", attn_probs, value_heads, preferred_element_type=jnp.float32
    )
    context = context.reshape(tokens, INNER).astype(jnp.bfloat16)
    return state + jnp.dot(context, w_out, preferred_element_type=jnp.float32)


def halves(value):
    high = value.astype(BF)
    return high, (value - high.astype(F32)).astype(BF)


def split_dot(left, right_high, right_low):
    rows = left.shape[0]
    high, low = halves(left)
    both = jnp.dot(jnp.concatenate([high, low], 0), right_high, preferred_element_type=F32)
    return both[:rows] + both[rows:] + jnp.dot(high, right_low, preferred_element_type=F32)


def in_vmem(*arrays):
    return tuple(pltpu.with_memory_space_constraint(a, pltpu.VMEM) for a in arrays)


def call(kernel, outs, n_in, flops, limit=40):
    return pl.pallas_call(
        kernel,
        out_shape=outs,
        in_specs=[IN_SMEM] + [IN_VMEM] * (n_in - 1),
        out_specs=jax.tree.map(lambda _: IN_VMEM, outs),
        compiler_params=pltpu.CompilerParams(vmem_limit_bytes=limit << 20),
        cost_estimate=pl.CostEstimate(flops=flops, bytes_accessed=1 << 20, transcendentals=0),
    )


def parts_kernel(core, own, other, b0_high, b0_low, b1_high, b1_low):
    first = core[0] == 0

    @pl.loop(0, own.shape[0] // 128)
    def _(block):
        rows = pl.ds(pl.multiple_of(block * 128, 128), 128)
        mine, theirs = own[rows, :], other[rows, :]
        b0_high[rows, :], b0_low[rows, :] = halves(jnp.where(first, mine, theirs))
        b1_high[rows, :], b1_low[rows, :] = halves(jnp.where(first, theirs, mine))


def product_kernel(core, own, other, b0_high, b0_low, b1_high, b1_low, c_high, c_low):
    @pl.loop(0, own.shape[0] // 256)
    def _(block):
        rows = pl.ds(pl.multiple_of(block * 256, 256), 256)
        high, low = b0_high[rows, :], b0_low[rows, :]
        both = jnp.dot(jnp.concatenate([high, low], 0), b1_high[...], preferred_element_type=F32)
        total = both[:256] + both[256:] + jnp.dot(high, b1_low[...], preferred_element_type=F32)
        total = total + (own[rows, :] + other[rows, :])
        c_high[rows, :], c_low[rows, :] = halves(total)


def source_kernel(core, mine, theirs, b1_high, b1_low, out):
    first = core[0] == 0
    half = out.shape[0]
    start = pl.multiple_of(core[0] * half, half)
    a, b = mine[pl.ds(start, half), :], theirs[pl.ds(start, half), :]
    r0, r1 = jnp.where(first, a, b), jnp.where(first, b, a)
    out[...] = r1 + r0 + split_dot(r0, b1_high[...], b1_low[...])


def squares_kernel(counted, mine, theirs, out):
    def tile(ref):
        total = jnp.zeros((8, ref.shape[1]), F32)
        for at in range(0, ref.shape[0], 8):
            total = total + ref[at : at + 8, :] * ref[at : at + 8, :]
        return sum(total[:, at : at + 128] for at in range(0, ref.shape[1], 128))

    zero = jnp.zeros(out.shape, F32)
    a = jnp.where(counted[0] == 1, tile(mine), zero)
    out[...] = a + jnp.where(counted[1] == 1, tile(theirs), zero)


def hop_kernel(chunk, active, received, before, source, c_high, c_low, sent, kept):
    rows = received.shape[0]
    mine = active[0] == 1

    @pl.when(mine)
    def _():
        e = received[...]
        kept[...] = e
        sent[...] = e + source[chunk * rows : (chunk + 1) * rows, :] + split_dot(e, c_high[...], c_low[...])

    @pl.when(jnp.logical_not(mine))
    def _():
        kept[...] = before[...]


def finish_kernel(core, own, other, r_other, b0_high, b0_low, b1_high, b1_low, w, c, state, u):
    half = own.shape[0]

    def rest(e):
        step = e + split_dot(e, b0_high[...], b0_low[...])

        @pl.when(core[0] == 0)
        def _():
            state[...] = w[...] + step
            u[...] = c[...] + e

        @pl.when(core[0] == 1)
        def _():
            x = step + r_other[...]
            u[...] = c[...] + x
            state[...] = w[...] + (x + split_dot(x, b1_high[...], b1_low[...]))

    first = core[0] == 0
    mine, theirs = own[...], other[...]
    rest(jnp.concatenate([jnp.where(first, mine, theirs), jnp.where(first, theirs, mine)], 0))


def per_device(c_states, w_query, w_key, w_value, w_out):
    c_guess = c_states[0]
    dev_index = lax.axis_index("depth")
    dev_count = lax.axis_size("depth")
    chips = dev_count // 2
    chip = dev_index // 2
    core = jnp.reshape(dev_index % 2, (1,)).astype(jnp.int32)
    tokens, width = c_guess.shape
    half = tokens // 2
    rows = half // CHUNKS
    swap_pairs = [(i, i ^ 1) for i in range(dev_count)]

    def swap(block):
        return lax.ppermute(block, "depth", swap_pairs)

    def f32_of(*shape):
        return pltpu.VMEM(shape, F32)

    square = pltpu.VMEM((width, width), BF)
    next_state = lax.ppermute(c_guess, "depth", [(i, i - 1) for i in range(1, dev_count)])
    own_map = 0.25 * jnp.dot(w_value[1], w_out[1], preferred_element_type=F32)
    other_map = swap(own_map)
    fine_f = apply_layer(c_guess, w_query[0], w_key[0], w_value[0], w_out[0])
    fine_c = apply_layer(fine_f, w_query[1], w_key[1], w_value[1], w_out[1])
    residual = fine_c - next_state

    own_map, other_map = in_vmem(own_map, other_map)
    maps = call(parts_kernel, (square,) * 4, 3, 1 << 22)(core, own_map, other_map)
    b0_high, b0_low, b1_high, b1_low = in_vmem(*maps)
    other_residual = swap(residual)
    source = call(source_kernel, f32_of(half, width), 5, 6 * half * width * width)(
        core, residual, other_residual, b1_high, b1_low
    )
    c_high, c_low = in_vmem(
        *call(product_kernel, (square,) * 2, 7, 6 * width**3)(
            core, own_map, other_map, b0_high, b0_low, b1_high, b1_low
        )
    )

    sent = [source[j * rows : (j + 1) * rows] for j in range(CHUNKS)]
    (source,) = in_vmem(source)
    kept = [jnp.zeros((rows, width), F32)] * CHUNKS
    flags = jnp.stack([dev_index, dev_index ^ 1]) < dev_count - 1
    flags = flags.astype(jnp.int32)
    for hop in range(chips - 1):
        if hop == 3:
            flags, sent[-1] = lax.optimization_barrier((flags, sent[-1]))
            total = call(squares_kernel, pltpu.VMEM((8, 128), F32), 3, 1 << 20)(flags, residual, other_residual)
            kept[0], total = lax.optimization_barrier((kept[0], total))
        if hop >= 4 and hop % 2 == 0 and 2 << (hop // 2 - 2) < dev_count:
            reach = 2 << (hop // 2 - 2)
            total, sent[-1] = lax.optimization_barrier((total, sent[-1]))
            total = total + lax.ppermute(total, "depth", [(i, i ^ reach) for i in range(dev_count)])
            kept[0], total = lax.optimization_barrier((kept[0], total))
        pairs = [(2 * hop + i, 2 * hop + 2 + i) for i in range(2)]
        active = jnp.reshape((chip == hop + 1).astype(jnp.int32), (1,))
        for j in range(CHUNKS):
            received = lax.ppermute(sent[j], "depth", pairs)
            if hop < chips - 2:
                sent[j], kept[j] = call(
                    functools.partial(hop_kernel, j),
                    (f32_of(rows, width), f32_of(rows, width)),
                    6,
                    6 * rows * width * width,
                )(active, received, kept[j], source, c_high, c_low)
            else:
                kept[j] = jnp.where(active[0] == 1, received, kept[j])
    own_e = jnp.concatenate(kept, 0)
    other_e = swap(own_e)
    new_state, corrected = call(
        finish_kernel, (f32_of(tokens, width), f32_of(tokens, width)), 10, 12 * tokens * width * width
    )(core, own_e, other_e, other_residual, b0_high, b0_low, b1_high, b1_low, fine_c, c_guess)
    relaxed = apply_layer(corrected, w_query[0], w_key[0], w_value[0], w_out[0])
    residual_rms = jnp.sqrt(jnp.sum(total) / ((dev_count - 1) * tokens * width)).reshape(1)
    return (jnp.stack([relaxed, new_state]), residual_rms)


def solution(mesh):
    in_specs = (
        P("depth", "dp", None),
        P("depth", None, None),
        P("depth", None, None),
        P("depth", None, None),
        P("depth", None, None),
    )
    out_specs = (P("depth", "dp", None), P("dp"))
    return jax.shard_map(
        per_device, mesh=mesh, in_specs=in_specs, out_specs=out_specs, check_vma=False
    )
```

time: 806 us -> 566 us (0.70)
  waiting for transfers between devices: 506 us -> 8.71 us
  starting transfers between devices: 42.5 us -> 371 us
  other arithmetic: 115 us -> 4.72 us
  Pallas kernels: 0 us -> 72.3 us
  blocking collectives: 70.6 us -> 0 us
  local copies, waits for them, and re-layouts: 7 us -> 55.9 us
  matrix products: 47.3 us -> 38.8 us
    ppermute x32 -> x68, waiting for transfers between devices: 506 us -> 8.71 us  [the longest x4 4.84 us: per_device(): lax.ppermute(total, 'depth', [(i, i ^ reach) for i in range(dev_count)])]
    ppermute x32 -> x68, starting transfers between devices: 42.5 us -> 371 us  [the longest x60 297 us: per_device(): received = lax.ppermute(sent[j], 'depth', pairs)]
    select_n x31 -> x4, other arithmetic: 108 us -> 0.97 us  [per_device(): kept[j] = jnp.where(active[0] == 1, received, kept[j])]
    pallas_call x0 -> x61, Pallas kernels: none -> 72.3 us  [the longest x56 49.4 us: per_device(): call(functools.partial(hop_kernel, j), (f32_of(rows, width), f32_of(rows,...]
    psum x1 -> x0, blocking collectives: 70.6 us -> none  [per_device(): total_sq = lax.psum(part_sq, 'depth')]
    unnamed x27 -> x150, local copies, waits for them, and re-layouts: 6.29 us -> 53.2 us
  transfers between devices with their start and end apart: 32 -> 68, of which waited for: 31 -> 4; matrix products, arithmetic and copies ran while one was open for 4% -> 5% of each run, Pallas kernels for 0% -> 12%
where the time goes in v1:
time: 566 us; the launch traced here: 556 us
  starting transfers between devices  371 us (66%)
  Pallas kernels  72.3 us (13%)
  local copies, waits for them, and re-layouts  55.9 us (10%)
  matrix products  38.8 us (7%)
  waiting for transfers between devices  8.71 us (2%)
    ppermute x60, starting transfers between devices, per_device(): received = lax.ppermute(sent[j], 'depth', pairs)  297 us
    ppermute x4, starting transfers between devices, per_device(): lax.ppermute(total, 'depth', [(i, i ^ reach) for i in range(dev_count)])  53.2 us
    unnamed x150, local copies, waits for them, and re-layouts  53.2 us
    pallas_call x56, Pallas kernels, per_device(): call(functools.partial(hop_kernel, j), (f32_of(rows, width), f32_of(rows,...  49.4 us
  transfers between devices with their start and end apart: 68, of which 4 were waited for; matrix products, arithmetic and copies ran while one was open for 5% of the time, Pallas kernels for 12%

profile of v1, /device:TPU:121, one launch (start us, length us, event | category | flops | bytes accessed | tf_op | source)
XLA Modules:
  0.0 556.1 jit_solution(10598055125092877925)
XLA Ops:
  0.6 6.7 %convolution_multiply_fusion.own = f32[1024,1024]{1,0:T(8,128)} fusion(bf16[2,1024,1024]{2,1,0:T(8,128)(2,1)} %param.9, bf16[2,1024,1024]{2,1,0:T(8,128)(2,1)} %param.8), kind=kOutput, calls=%fused_computation.3 | convolution fusion | flops 2148532224 | bytes 8388608 | tf_op jit(solution)/shard_map/dot_general | solution.py:175
  7.3 9.2 %collective-permute-start.2 = (f32[1024,1024]{1,0:T(8,128)}, f32[1024,1024]{1,0:T(8,128)}, u32[]{:S(2)}, u32[]{:S(2)}) collective-permute-start(f32[1024,1024]{1,0:T(8,128)} %convolution_multiply_fusion.own), channel_id=1, source_target_pairs={{0,1},{1,0},{2,3},{3,2},{4,5},{5,4},{6,7},{7,6},{8,9},{9,8},{10,11... | collective-permute-start | bytes 12582920 | tf_op jit(solution)/shard_map/ppermute | solution.py:168
  16.5 11.1 %collective-permute-start = (f32[256,1024]{1,0:T(8,128)S(1)}, f32[256,1024]{1,0:T(8,128)}, u32[]{:S(2)}, u32[]{:S(2)}) collective-permute-start(f32[256,1024]{1,0:T(8,128)S(1)} %bitcast.211), channel_id=1, source_target_pairs={{1,0},{2,1},{3,2},{4,3},{5,4},{6,5},{7,6},{8,7},{9,8},{10,9},{11,1... | collective-permute-start | bytes 3145736 | tf_op jit(solution)/shard_map/ppermute | solution.py:174
  28.2 2.5 fusion.58
  33.1 2.1 fusion.162
  35.2 2.1 convolution_convert_fusion.2
  45.4 3.1 fusion.88
  48.5 3.3 fusion.168
  51.8 2.1 convolution_convert_fusion.1
  54.6 2.9 fusion.173
  57.6 5.4 shard_map.68
  68.6 10.9 %shard_map.70 = (bf16[1024,1024]{1,0:T(8,128)(2,1)S(1)}, bf16[1024,1024]{1,0:T(8,128)(2,1)S(1)}) custom-call(s32[1]{0:T(128)} %bitcast.core, f32[1024,1024]{1,0:T(8,128)} %convolution_multiply_fusion.own, f32[1024,1024]{1,0:T(8,128)} %collective-permute-done.2.other, bf16[1024,1024]{1,0:T(8,128)(2,1)S(1)} %get-tuple-element.144.b0_high, ...), custom_call_target="tpu_custom_call" | custom-call | flops 6442450944 | bytes 1048576 | tf_op jit(solution)/shard_map/pallas_call | solution.py:189
  85.0 1.6 copy-done.1
  117.4 17.7 %collective-permute-start.12 = (f32[8,128]{1,0:T(8,128)S(1)}, f32[8,128]{1,0:T(8,128)S(1)}, u32[]{:S(2)}, u32[]{:S(2)}) collective-permute-start(f32[8,128]{1,0:T(8,128)S(1)} %shard_map.77), channel_id=1, source_target_pairs={{0,2},{1,3},{2,0},{3,1},{4,6},{5,7},{6,4},{7,5},{8,10},{9,11},{10,... | collective-permute-start | bytes 12296 | tf_op jit(solution)/shard_map/ppermute | solution.py:207
  136.6 1.6 copy-done.5
  143.0 1.6 shard_map.82
  146.6 1.6 copy-done.6
  155.1 16.1 %collective-permute-start.17 = (f32[8,128]{1,0:T(8,128)S(1)}, f32[8,128]{1,0:T(8,128)S(1)}, u32[]{:S(2)}, u32[]{:S(2)}) collective-permute-start(f32[8,128]{1,0:T(8,128)S(1)} %add.55), channel_id=1, source_target_pairs={{0,4},{1,5},{2,6},{3,7},{4,0},{5,1},{6,2},{7,3},{8,12},{9,13},{10,... | collective-permute-start | bytes 12296 | tf_op jit(solution)/shard_map/ppermute | solution.py:207
  171.2 2.0 collective-permute-done.17
  173.3 1.6 copy-done.7
  179.5 1.6 shard_map.86
  183.1 1.6 copy-done.8
  188.1 17.3 %collective-permute-start.55 = (f32[32,1024]{1,0:T(8,128)}, f32[32,1024]{1,0:T(8,128)S(1)}, u32[]{:S(2)}, u32[]{:S(2)}) collective-permute-start(f32[32,1024]{1,0:T(8,128)} %get-tuple-element.255), channel_id=1, source_target_pairs={{16,18},{17,19},{48,50},{49,51},{80,82},{81,83},{112,114},{113,115}} | collective-permute-start | bytes 393224 | tf_op jit(solution)/shard_map/ppermute | solution.py:212
  208.3 9.1 %collective-permute-start.22 = (f32[8,128]{1,0:T(8,128)S(1)}, f32[8,128]{1,0:T(8,128)S(1)}, u32[]{:S(2)}, u32[]{:S(2)}) collective-permute-start(f32[8,128]{1,0:T(8,128)S(1)} %add.56), channel_id=1, source_target_pairs={{0,8},{1,9},{2,10},{3,11},{4,12},{5,13},{6,14},{7,15},{8,0},{9,1},... | collective-permute-start | bytes 12296 | tf_op jit(solution)/shard_map/ppermute | solution.py:207
  220.9 11.9 %collective-permute-start.23 = (f32[32,1024]{1,0:T(8,128)}, f32[32,1024]{1,0:T(8,128)}, u32[]{:S(2)}, u32[]{:S(2)}) collective-permute-start(f32[32,1024]{1,0:T(8,128)} %get-tuple-element.193), channel_id=1, source_target_pairs={{18,20},{19,21},{50,52},{51,53},{82,84},{83,85},{114,116},{115,117}} | collective-permute-start | bytes 393224 | tf_op jit(solution)/shard_map/ppermute | solution.py:212
  233.5 10.2 %collective-permute-start.41 = (f32[32,1024]{1,0:T(8,128)}, f32[32,1024]{1,0:T(8,128)}, u32[]{:S(2)}, u32[]{:S(2)}) collective-permute-start(f32[32,1024]{1,0:T(8,128)} %get-tuple-element.229), channel_id=1, source_target_pairs={{18,20},{19,21},{50,52},{51,53},{82,84},{83,85},{114,116},{115,117}} | collective-permute-start | bytes 393224 | tf_op jit(solution)/shard_map/ppermute | solution.py:212
  244.3 9.5 %collective-permute-start.56 = (f32[32,1024]{1,0:T(8,128)}, f32[32,1024]{1,0:T(8,128)S(1)}, u32[]{:S(2)}, u32[]{:S(2)}) collective-permute-start(f32[32,1024]{1,0:T(8,128)} %get-tuple-element.257), channel_id=1, source_target_pairs={{18,20},{19,21},{50,52},{51,53},{82,84},{83,85},{114,116},{115,117}} | collective-permute-start | bytes 393224 | tf_op jit(solution)/shard_map/ppermute | solution.py:212
  253.9 1.6 shard_map.90
  255.5 10.2 %collective-permute-start.26 = (f32[32,1024]{1,0:T(8,128)}, f32[32,1024]{1,0:T(8,128)}, u32[]{:S(2)}, u32[]{:S(2)}) collective-permute-start(f32[32,1024]{1,0:T(8,128)} %get-tuple-element.200), channel_id=1, source_target_pairs={{18,20},{19,21},{50,52},{51,53},{82,84},{83,85},{114,116},{115,117}} | collective-permute-start | bytes 393224 | tf_op jit(solution)/shard_map/ppermute | solution.py:212
  265.6 1.6 copy-done.10
  268.8 9.7 %collective-permute-start.24 = (f32[32,1024]{1,0:T(8,128)}, f32[32,1024]{1,0:T(8,128)S(1)}, u32[]{:S(2)}, u32[]{:S(2)}) collective-permute-start(f32[32,1024]{1,0:T(8,128)} %get-tuple-element.195), channel_id=1, source_target_pairs={{20,22},{21,23},{52,54},{53,55},{84,86},{85,87},{116,118},{117,119}} | collective-permute-start | bytes 393224 | tf_op jit(solution)/shard_map/ppermute | solution.py:212
  278.5 1.8 shard_map.105
  280.3 11.0 %collective-permute-start.42 = (f32[32,1024]{1,0:T(8,128)}, f32[32,1024]{1,0:T(8,128)S(1)}, u32[]{:S(2)}, u32[]{:S(2)}) collective-permute-start(f32[32,1024]{1,0:T(8,128)} %get-tuple-element.231), channel_id=1, source_target_pairs={{20,22},{21,23},{52,54},{53,55},{84,86},{85,87},{116,118},{117,119}} | collective-permute-start | bytes 393224 | tf_op jit(solution)/shard_map/ppermute | solution.py:212
  292.0 11.0 %collective-permute-start.57 = (f32[32,1024]{1,0:T(8,128)}, f32[32,1024]{1,0:T(8,128)S(1)}, u32[]{:S(2)}, u32[]{:S(2)}) collective-permute-start(f32[32,1024]{1,0:T(8,128)} %get-tuple-element.259), channel_id=1, source_target_pairs={{20,22},{21,23},{52,54},{53,55},{84,86},{85,87},{116,118},{117,119}} | collective-permute-start | bytes 393224 | tf_op jit(solution)/shard_map/ppermute | solution.py:212
  304.5 10.4 %collective-permute-start.27 = (f32[8,128]{1,0:T(8,128)S(1)}, f32[8,128]{1,0:T(8,128)S(1)}, u32[]{:S(2)}, u32[]{:S(2)}) collective-permute-start(f32[8,128]{1,0:T(8,128)S(1)} %add.57), channel_id=1, source_target_pairs={{0,16},{1,17},{2,18},{3,19},{4,20},{5,21},{6,22},{7,23},{8,24},{9,... | collective-permute-start | bytes 12296 | tf_op jit(solution)/shard_map/ppermute | solution.py:207
  314.9 10.2 %collective-permute-start.62 = (f32[32,1024]{1,0:T(8,128)}, f32[32,1024]{1,0:T(8,128)}, u32[]{:S(2)}, u32[]{:S(2)}) collective-permute-start(f32[32,1024]{1,0:T(8,128)} %copy-done.64), channel_id=1, source_target_pairs={{20,22},{21,23},{52,54},{53,55},{84,86},{85,87},{116,118},{117,119}} | collective-permute-start | bytes 393224 | tf_op jit(solution)/shard_map/ppermute | solution.py:212
  328.0 10.2 %collective-permute-start.28 = (f32[32,1024]{1,0:T(8,128)}, f32[32,1024]{1,0:T(8,128)S(1)}, u32[]{:S(2)}, u32[]{:S(2)}) collective-permute-start(f32[32,1024]{1,0:T(8,128)} %get-tuple-element.205), channel_id=1, source_target_pairs={{22,24},{23,25},{54,56},{55,57},{86,88},{87,89},{118,120},{119,121}} | collective-permute-start | bytes 393224 | tf_op jit(solution)/shard_map/ppermute | solution.py:212
  340.4 11.4 %collective-permute-start.43 = (f32[32,1024]{1,0:T(8,128)}, f32[32,1024]{1,0:T(8,128)}, u32[]{:S(2)}, u32[]{:S(2)}) collective-permute-start(f32[32,1024]{1,0:T(8,128)} %get-tuple-element.233), channel_id=1, source_target_pairs={{22,24},{23,25},{54,56},{55,57},{86,88},{87,89},{118,120},{119,121}} | collective-permute-start | bytes 393224 | tf_op jit(solution)/shard_map/ppermute | solution.py:212
  352.5 11.4 %collective-permute-start.58 = (f32[32,1024]{1,0:T(8,128)}, f32[32,1024]{1,0:T(8,128)}, u32[]{:S(2)}, u32[]{:S(2)}) collective-permute-start(f32[32,1024]{1,0:T(8,128)} %get-tuple-element.261), channel_id=1, source_target_pairs={{22,24},{23,25},{54,56},{55,57},{86,88},{87,89},{118,120},{119,121}} | collective-permute-start | bytes 393224 | tf_op jit(solution)/shard_map/ppermute | solution.py:212
  363.9 1.6 shard_map.124
  365.5 11.4 %collective-permute-start.63 = (f32[32,1024]{1,0:T(8,128)}, f32[32,1024]{1,0:T(8,128)}, u32[]{:S(2)}, u32[]{:S(2)}) collective-permute-start(f32[32,1024]{1,0:T(8,128)} %get-tuple-element.271), channel_id=1, source_target_pairs={{22,24},{23,25},{54,56},{55,57},{86,88},{87,89},{118,120},{119,121}} | collective-permute-start | bytes 393224 | tf_op jit(solution)/shard_map/ppermute | solution.py:212
  377.6 9.9 %collective-permute-start.29 = (f32[32,1024]{1,0:T(8,128)}, f32[32,1024]{1,0:T(8,128)S(1)}, u32[]{:S(2)}, u32[]{:S(2)}) collective-permute-start(f32[32,1024]{1,0:T(8,128)} %get-tuple-element.207), channel_id=1, source_target_pairs={{24,26},{25,27},{56,58},{57,59},{88,90},{89,91},{120,122},{121,123}} | collective-permute-start | bytes 393224 | tf_op jit(solution)/shard_map/ppermute | solution.py:212
  390.7 10.2 %collective-permute-start.44 = (f32[32,1024]{1,0:T(8,128)}, f32[32,1024]{1,0:T(8,128)}, u32[]{:S(2)}, u32[]{:S(2)}) collective-permute-start(f32[32,1024]{1,0:T(8,128)} %get-tuple-element.235), channel_id=1, source_target_pairs={{24,26},{25,27},{56,58},{57,59},{88,90},{89,91},{120,122},{121,123}} | collective-permute-start | bytes 393224 | tf_op jit(solution)/shard_map/ppermute | solution.py:212
  402.5 10.2 %collective-permute-start.59 = (f32[32,1024]{1,0:T(8,128)}, f32[32,1024]{1,0:T(8,128)}, u32[]{:S(2)}, u32[]{:S(2)}) collective-permute-start(f32[32,1024]{1,0:T(8,128)} %get-tuple-element.263), channel_id=1, source_target_pairs={{24,26},{25,27},{56,58},{57,59},{88,90},{89,91},{120,122},{121,123}} | collective-permute-start | bytes 393224 | tf_op jit(solution)/shard_map/ppermute | solution.py:212
  414.2 9.5 %collective-permute-start.64 = (f32[32,1024]{1,0:T(8,128)}, f32[32,1024]{1,0:T(8,128)S(1)}, u32[]{:S(2)}, u32[]{:S(2)}) collective-permute-start(f32[32,1024]{1,0:T(8,128)} %get-tuple-element.273), channel_id=1, source_target_pairs={{24,26},{25,27},{56,58},{57,59},{88,90},{89,91},{120,122},{121,123}} | collective-permute-start | bytes 393224 | tf_op jit(solution)/shard_map/ppermute | solution.py:212
  424.5 10.2 %collective-permute-start.30 = (f32[32,1024]{1,0:T(8,128)}, f32[32,1024]{1,0:T(8,128)}, u32[]{:S(2)}, u32[]{:S(2)}) collective-permute-start(f32[32,1024]{1,0:T(8,128)} %get-tuple-element.209), channel_id=1, source_target_pairs={{26,28},{27,29},{58,60},{59,61},{90,92},{91,93},{122,124},{123,125}} | collective-permute-start | bytes 393224 | tf_op jit(solution)/shard_map/ppermute | solution.py:212
  434.6 1.6 copy-done.14
  437.8 9.5 %collective-permute-start.45 = (f32[32,1024]{1,0:T(8,128)}, f32[32,1024]{1,0:T(8,128)S(1)}, u32[]{:S(2)}, u32[]{:S(2)}) collective-permute-start(f32[32,1024]{1,0:T(8,128)} %get-tuple-element.237), channel_id=1, source_target_pairs={{26,28},{27,29},{58,60},{59,61},{90,92},{91,93},{122,124},{123,125}} | collective-permute-start | bytes 393224 | tf_op jit(solution)/shard_map/ppermute | solution.py:212
  448.9 9.5 %collective-permute-start.60 = (f32[32,1024]{1,0:T(8,128)}, f32[32,1024]{1,0:T(8,128)S(1)}, u32[]{:S(2)}, u32[]{:S(2)}) collective-permute-start(f32[32,1024]{1,0:T(8,128)} %get-tuple-element.265), channel_id=1, source_target_pairs={{26,28},{27,29},{58,60},{59,61},{90,92},{91,93},{122,124},{123,125}} | collective-permute-start | bytes 393224 | tf_op jit(solution)/shard_map/ppermute | solution.py:212
  460.7 9.5 %collective-permute-start.65 = (f32[32,1024]{1,0:T(8,128)}, f32[32,1024]{1,0:T(8,128)S(1)}, u32[]{:S(2)}, u32[]{:S(2)}) collective-permute-start(f32[32,1024]{1,0:T(8,128)} %get-tuple-element.275), channel_id=1, source_target_pairs={{26,28},{27,29},{58,60},{59,61},{90,92},{91,93},{122,124},{123,125}} | collective-permute-start | bytes 393224 | tf_op jit(solution)/shard_map/ppermute | solution.py:212
  472.4 10.3 %collective-permute-start.31 = (f32[32,1024]{1,0:T(8,128)}, f32[32,1024]{1,0:T(8,128)}, u32[]{:S(2)}, u32[]{:S(2)}) collective-permute-start(f32[32,1024]{1,0:T(8,128)} %get-tuple-element.211), channel_id=1, source_target_pairs={{28,30},{29,31},{60,62},{61,63},{92,94},{93,95},{124,126},{125,127}} | collective-permute-start | bytes 393224 | tf_op jit(solution)/shard_map/ppermute | solution.py:212
  482.8 1.6 copy-done.15
  484.4 11.6 %collective-permute-start.46 = (f32[32,1024]{1,0:T(8,128)S(1)}, f32[32,1024]{1,0:T(8,128)S(1)}, u32[]{:S(2)}, u32[]{:S(2)}) collective-permute-start(f32[32,1024]{1,0:T(8,128)S(1)} %get-tuple-element.239), channel_id=1, source_target_pairs={{28,30},{29,31},{60,62},{61,63},{92,94},{93,95},{124,126},{125,127}} | collective-permute-start | bytes 393224 | tf_op jit(solution)/shard_map/ppermute | solution.py:212
  496.0 11.0 %collective-permute-start.61 = (f32[32,1024]{1,0:T(8,128)S(1)}, f32[32,1024]{1,0:T(8,128)S(1)}, u32[]{:S(2)}, u32[]{:S(2)}) collective-permute-start(f32[32,1024]{1,0:T(8,128)S(1)} %get-tuple-element.267), channel_id=1, source_target_pairs={{28,30},{29,31},{60,62},{61,63},{92,94},{93,95},{124,126},{125,127}} | collective-permute-start | bytes 393224 | tf_op jit(solution)/shard_map/ppermute | solution.py:212
  507.0 11.1 %collective-permute-start.66 = (f32[32,1024]{1,0:T(8,128)S(1)}, f32[32,1024]{1,0:T(8,128)S(1)}, u32[]{:S(2)}, u32[]{:S(2)}) collective-permute-start(f32[32,1024]{1,0:T(8,128)S(1)} %get-tuple-element.277), channel_id=1, source_target_pairs={{28,30},{29,31},{60,62},{61,63},{92,94},{93,95},{124,126},{125,127}} | collective-permute-start | bytes 393224 | tf_op jit(solution)/shard_map/ppermute | solution.py:212
  519.1 3.7 collective-permute-done.66
  527.0 1.6 copy-done.22
  528.6 1.6 copy-done.24
  530.2 1.6 copy-done.27
  531.8 1.6 copy-done.29
  535.5 4.9 shard_map.128
  542.0 2.5 fusion.91
  546.9 2.1 fusion.174
  549.0 2.1 convolution_convert_fusion
  (333 shorter events, 124.8 us)
Async XLA Ops:
  7.3 50.3 %collective-permute-start.2 = (f32[1024,1024]{1,0:T(8,128)}, f32[1024,1024]{1,0:T(8,128)}, u32[]{:S(2)}, u32[]{:S(2)}) collective-permute-start(f32[1024,1024]{1,0:T(8,128)} %convolution_multiply_fusion.own), channel_id=1, source_target_pairs={{0,1},{1,0},{2,3},{3,2},{4,5},{5,4},{6,7},{7,6},{8,9},{9,8},{10,11... | collective-permute-start | bytes 12582920 | tf_op jit(solution)/shard_map/ppermute | solution.py:168
  16.5 37.4 %collective-permute-start = (f32[256,1024]{1,0:T(8,128)S(1)}, f32[256,1024]{1,0:T(8,128)}, u32[]{:S(2)}, u32[]{:S(2)}) collective-permute-start(f32[256,1024]{1,0:T(8,128)S(1)} %bitcast.211), channel_id=1, source_target_pairs={{1,0},{2,1},{3,2},{4,3},{5,4},{6,5},{7,6},{8,7},{9,8},{10,9},{11,1... | collective-permute-start | bytes 3145736 | tf_op jit(solution)/shard_map/ppermute | solution.py:174
  57.5 5.4 collective-permute-start.1
  65.5 19.5 %collective-permute-start.7 = (f32[32,1024]{1,0:T(8,128)S(1)}, f32[32,1024]{1,0:T(8,128)S(1)}, u32[]{:S(2)}, u32[]{:S(2)}) collective-permute-start(f32[32,1024]{1,0:T(8,128)S(1)} %get-tuple-element.284), channel_id=1, source_target_pairs={{0,2},{1,3},{32,34},{33,35},{64,66},{65,67},{96,98},{97,99}} | collective-permute-start | bytes 393224 | tf_op jit(solution)/shard_map/ppermute | solution.py:212
  66.1 16.2 %collective-permute-start.3 = (f32[32,1024]{1,0:T(8,128)S(1)}, f32[32,1024]{1,0:T(8,128)S(1)}, u32[]{:S(2)}, u32[]{:S(2)}) collective-permute-start(f32[32,1024]{1,0:T(8,128)S(1)} %get-tuple-element.285), channel_id=1, source_target_pairs={{0,2},{1,3},{32,34},{33,35},{64,66},{65,67},{96,98},{97,99}} | collective-permute-start | bytes 393224 | tf_op jit(solution)/shard_map/ppermute | solution.py:212
  66.8 21.1 %collective-permute-start.32 = (f32[32,1024]{1,0:T(8,128)}, f32[32,1024]{1,0:T(8,128)S(1)}, u32[]{:S(2)}, u32[]{:S(2)}) collective-permute-start(f32[32,1024]{1,0:T(8,128)} %get-tuple-element.282), channel_id=1, source_target_pairs={{0,2},{1,3},{32,34},{33,35},{64,66},{65,67},{96,98},{97,99}} | collective-permute-start | bytes 393224 | tf_op jit(solution)/shard_map/ppermute | solution.py:212
  67.5 24.0 %collective-permute-start.47 = (f32[32,1024]{1,0:T(8,128)}, f32[32,1024]{1,0:T(8,128)S(1)}, u32[]{:S(2)}, u32[]{:S(2)}) collective-permute-start(f32[32,1024]{1,0:T(8,128)} %get-tuple-element.283), channel_id=1, source_target_pairs={{0,2},{1,3},{32,34},{33,35},{64,66},{65,67},{96,98},{97,99}} | collective-permute-start | bytes 393224 | tf_op jit(solution)/shard_map/ppermute | solution.py:212
  83.7 9.1 %collective-permute-start.4 = (f32[32,1024]{1,0:T(8,128)}, f32[32,1024]{1,0:T(8,128)}, u32[]{:S(2)}, u32[]{:S(2)}) collective-permute-start(f32[32,1024]{1,0:T(8,128)} %get-tuple-element.148), channel_id=1, source_target_pairs={{2,4},{3,5},{34,36},{35,37},{66,68},{67,69},{98,100},{99,101}} | collective-permute-start | bytes 393224 | tf_op jit(solution)/shard_map/ppermute | solution.py:212
  87.2 7.8 %collective-permute-start.8 = (f32[32,1024]{1,0:T(8,128)}, f32[32,1024]{1,0:T(8,128)S(1)}, u32[]{:S(2)}, u32[]{:S(2)}) collective-permute-start(f32[32,1024]{1,0:T(8,128)} %get-tuple-element.154), channel_id=1, source_target_pairs={{2,4},{3,5},{34,36},{35,37},{66,68},{67,69},{98,100},{99,101}} | collective-permute-start | bytes 393224 | tf_op jit(solution)/shard_map/ppermute | solution.py:212
  90.2 7.2 %collective-permute-start.33 = (f32[32,1024]{1,0:T(8,128)}, f32[32,1024]{1,0:T(8,128)}, u32[]{:S(2)}, u32[]{:S(2)}) collective-permute-start(f32[32,1024]{1,0:T(8,128)} %get-tuple-element.213), channel_id=1, source_target_pairs={{2,4},{3,5},{34,36},{35,37},{66,68},{67,69},{98,100},{99,101}} | collective-permute-start | bytes 393224 | tf_op jit(solution)/shard_map/ppermute | solution.py:212
  92.1 6.8 %collective-permute-start.48 = (f32[32,1024]{1,0:T(8,128)}, f32[32,1024]{1,0:T(8,128)S(1)}, u32[]{:S(2)}, u32[]{:S(2)}) collective-permute-start(f32[32,1024]{1,0:T(8,128)} %get-tuple-element.241), channel_id=1, source_target_pairs={{2,4},{3,5},{34,36},{35,37},{66,68},{67,69},{98,100},{99,101}} | collective-permute-start | bytes 393224 | tf_op jit(solution)/shard_map/ppermute | solution.py:212
  96.7 7.1 %collective-permute-start.9 = (f32[32,1024]{1,0:T(8,128)S(1)}, f32[32,1024]{1,0:T(8,128)S(1)}, u32[]{:S(2)}, u32[]{:S(2)}) collective-permute-start(f32[32,1024]{1,0:T(8,128)S(1)} %get-tuple-element.156), channel_id=1, source_target_pairs={{4,6},{5,7},{36,38},{37,39},{68,70},{69,71},{100,102},{101,103}} | collective-permute-start | bytes 393224 | tf_op jit(solution)/shard_map/ppermute | solution.py:212
  100.3 9.2 %collective-permute-start.6 = (f32[32,1024]{1,0:T(8,128)}, f32[32,1024]{1,0:T(8,128)S(1)}, u32[]{:S(2)}, u32[]{:S(2)}) collective-permute-start(f32[32,1024]{1,0:T(8,128)} %get-tuple-element.152), channel_id=1, source_target_pairs={{6,8},{7,9},{38,40},{39,41},{70,72},{71,73},{102,104},{103,105}} | collective-permute-start | bytes 393224 | tf_op jit(solution)/shard_map/ppermute | solution.py:212
  101.7 10.0 %collective-permute-start.35 = (f32[32,1024]{1,0:T(8,128)}, f32[32,1024]{1,0:T(8,128)S(1)}, u32[]{:S(2)}, u32[]{:S(2)}) collective-permute-start(f32[32,1024]{1,0:T(8,128)} %get-tuple-element.217), channel_id=1, source_target_pairs={{6,8},{7,9},{38,40},{39,41},{70,72},{71,73},{102,104},{103,105}} | collective-permute-start | bytes 393224 | tf_op jit(solution)/shard_map/ppermute | solution.py:212
  103.1 10.0 %collective-permute-start.50 = (f32[32,1024]{1,0:T(8,128)}, f32[32,1024]{1,0:T(8,128)S(1)}, u32[]{:S(2)}, u32[]{:S(2)}) collective-permute-start(f32[32,1024]{1,0:T(8,128)} %get-tuple-element.245), channel_id=1, source_target_pairs={{6,8},{7,9},{38,40},{39,41},{70,72},{71,73},{102,104},{103,105}} | collective-permute-start | bytes 393224 | tf_op jit(solution)/shard_map/ppermute | solution.py:212
  105.1 9.4 %collective-permute-start.11 = (f32[32,1024]{1,0:T(8,128)}, f32[32,1024]{1,0:T(8,128)}, u32[]{:S(2)}, u32[]{:S(2)}) collective-permute-start(f32[32,1024]{1,0:T(8,128)} %get-tuple-element.164), channel_id=1, source_target_pairs={{6,8},{7,9},{38,40},{39,41},{70,72},{71,73},{102,104},{103,105}} | collective-permute-start | bytes 393224 | tf_op jit(solution)/shard_map/ppermute | solution.py:212
  111.1 25.5 %collective-permute-start.10 = (f32[32,1024]{1,0:T(8,128)}, f32[32,1024]{1,0:T(8,128)S(1)}, u32[]{:S(2)}, u32[]{:S(2)}) collective-permute-start(f32[32,1024]{1,0:T(8,128)} %get-tuple-element.161), channel_id=1, source_target_pairs={{8,10},{9,11},{40,42},{41,43},{72,74},{73,75},{104,106},{105,107}} | collective-permute-start | bytes 393224 | tf_op jit(solution)/shard_map/ppermute | solution.py:212
  112.4 27.0 %collective-permute-start.36 = (f32[32,1024]{1,0:T(8,128)}, f32[32,1024]{1,0:T(8,128)S(1)}, u32[]{:S(2)}, u32[]{:S(2)}) collective-permute-start(f32[32,1024]{1,0:T(8,128)} %get-tuple-element.219), channel_id=1, source_target_pairs={{8,10},{9,11},{40,42},{41,43},{72,74},{73,75},{104,106},{105,107}} | collective-permute-start | bytes 393224 | tf_op jit(solution)/shard_map/ppermute | solution.py:212
  113.8 27.0 %collective-permute-start.51 = (f32[32,1024]{1,0:T(8,128)}, f32[32,1024]{1,0:T(8,128)S(1)}, u32[]{:S(2)}, u32[]{:S(2)}) collective-permute-start(f32[32,1024]{1,0:T(8,128)} %get-tuple-element.247), channel_id=1, source_target_pairs={{8,10},{9,11},{40,42},{41,43},{72,74},{73,75},{104,106},{105,107}} | collective-permute-start | bytes 393224 | tf_op jit(solution)/shard_map/ppermute | solution.py:212
  116.1 26.9 %collective-permute-start.15 = (f32[32,1024]{1,0:T(8,128)}, f32[32,1024]{1,0:T(8,128)}, u32[]{:S(2)}, u32[]{:S(2)}) collective-permute-start(f32[32,1024]{1,0:T(8,128)} %get-tuple-element.174), channel_id=1, source_target_pairs={{8,10},{9,11},{40,42},{41,43},{72,74},{73,75},{104,106},{105,107}} | collective-permute-start | bytes 393224 | tf_op jit(solution)/shard_map/ppermute | solution.py:212
  117.4 19.2 %collective-permute-start.12 = (f32[8,128]{1,0:T(8,128)S(1)}, f32[8,128]{1,0:T(8,128)S(1)}, u32[]{:S(2)}, u32[]{:S(2)}) collective-permute-start(f32[8,128]{1,0:T(8,128)S(1)} %shard_map.77), channel_id=1, source_target_pairs={{0,2},{1,3},{2,0},{3,1},{4,6},{5,7},{6,4},{7,5},{8,10},{9,11},{10,... | collective-permute-start | bytes 12296 | tf_op jit(solution)/shard_map/ppermute | solution.py:207
  138.8 7.8 %collective-permute-start.13 = (f32[32,1024]{1,0:T(8,128)}, f32[32,1024]{1,0:T(8,128)S(1)}, u32[]{:S(2)}, u32[]{:S(2)}) collective-permute-start(f32[32,1024]{1,0:T(8,128)} %get-tuple-element.169), channel_id=1, source_target_pairs={{10,12},{11,13},{42,44},{43,45},{74,76},{75,77},{106,108},{107,109}} | collective-permute-start | bytes 393224 | tf_op jit(solution)/shard_map/ppermute | solution.py:212
  140.2 9.3 %collective-permute-start.37 = (f32[32,1024]{1,0:T(8,128)}, f32[32,1024]{1,0:T(8,128)S(1)}, u32[]{:S(2)}, u32[]{:S(2)}) collective-permute-start(f32[32,1024]{1,0:T(8,128)} %get-tuple-element.221), channel_id=1, source_target_pairs={{10,12},{11,13},{42,44},{43,45},{74,76},{75,77},{106,108},{107,109}} | collective-permute-start | bytes 393224 | tf_op jit(solution)/shard_map/ppermute | solution.py:212
  142.3 8.5 %collective-permute-start.52 = (f32[32,1024]{1,0:T(8,128)}, f32[32,1024]{1,0:T(8,128)S(1)}, u32[]{:S(2)}, u32[]{:S(2)}) collective-permute-start(f32[32,1024]{1,0:T(8,128)} %get-tuple-element.249), channel_id=1, source_target_pairs={{10,12},{11,13},{42,44},{43,45},{74,76},{75,77},{106,108},{107,109}} | collective-permute-start | bytes 393224 | tf_op jit(solution)/shard_map/ppermute | solution.py:212
  145.3 6.9 %collective-permute-start.16 = (f32[32,1024]{1,0:T(8,128)}, f32[32,1024]{1,0:T(8,128)}, u32[]{:S(2)}, u32[]{:S(2)}) collective-permute-start(f32[32,1024]{1,0:T(8,128)} %get-tuple-element.176), channel_id=1, source_target_pairs={{10,12},{11,13},{42,44},{43,45},{74,76},{75,77},{106,108},{107,109}} | collective-permute-start | bytes 393224 | tf_op jit(solution)/shard_map/ppermute | solution.py:212
  148.8 24.4 %collective-permute-start.14 = (f32[32,1024]{1,0:T(8,128)}, f32[32,1024]{1,0:T(8,128)S(1)}, u32[]{:S(2)}, u32[]{:S(2)}) collective-permute-start(f32[32,1024]{1,0:T(8,128)} %get-tuple-element.171), channel_id=1, source_target_pairs={{12,14},{13,15},{44,46},{45,47},{76,78},{77,79},{108,110},{109,111}} | collective-permute-start | bytes 393224 | tf_op jit(solution)/shard_map/ppermute | solution.py:212
  150.2 26.0 %collective-permute-start.38 = (f32[32,1024]{1,0:T(8,128)}, f32[32,1024]{1,0:T(8,128)S(1)}, u32[]{:S(2)}, u32[]{:S(2)}) collective-permute-start(f32[32,1024]{1,0:T(8,128)} %get-tuple-element.223), channel_id=1, source_target_pairs={{12,14},{13,15},{44,46},{45,47},{76,78},{77,79},{108,110},{109,111}} | collective-permute-start | bytes 393224 | tf_op jit(solution)/shard_map/ppermute | solution.py:212
  151.6 26.0 %collective-permute-start.53 = (f32[32,1024]{1,0:T(8,128)}, f32[32,1024]{1,0:T(8,128)S(1)}, u32[]{:S(2)}, u32[]{:S(2)}) collective-permute-start(f32[32,1024]{1,0:T(8,128)} %get-tuple-element.251), channel_id=1, source_target_pairs={{12,14},{13,15},{44,46},{45,47},{76,78},{77,79},{108,110},{109,111}} | collective-permute-start | bytes 393224 | tf_op jit(solution)/shard_map/ppermute | solution.py:212
  153.8 25.7 %collective-permute-start.20 = (f32[32,1024]{1,0:T(8,128)}, f32[32,1024]{1,0:T(8,128)}, u32[]{:S(2)}, u32[]{:S(2)}) collective-permute-start(f32[32,1024]{1,0:T(8,128)} %get-tuple-element.186), channel_id=1, source_target_pairs={{12,14},{13,15},{44,46},{45,47},{76,78},{77,79},{108,110},{109,111}} | collective-permute-start | bytes 393224 | tf_op jit(solution)/shard_map/ppermute | solution.py:212
  155.1 18.1 %collective-permute-start.17 = (f32[8,128]{1,0:T(8,128)S(1)}, f32[8,128]{1,0:T(8,128)S(1)}, u32[]{:S(2)}, u32[]{:S(2)}) collective-permute-start(f32[8,128]{1,0:T(8,128)S(1)} %add.55), channel_id=1, source_target_pairs={{0,4},{1,5},{2,6},{3,7},{4,0},{5,1},{6,2},{7,3},{8,12},{9,13},{10,... | collective-permute-start | bytes 12296 | tf_op jit(solution)/shard_map/ppermute | solution.py:207
  175.5 7.6 %collective-permute-start.18 = (f32[32,1024]{1,0:T(8,128)}, f32[32,1024]{1,0:T(8,128)S(1)}, u32[]{:S(2)}, u32[]{:S(2)}) collective-permute-start(f32[32,1024]{1,0:T(8,128)} %get-tuple-element.181), channel_id=1, source_target_pairs={{14,16},{15,17},{46,48},{47,49},{78,80},{79,81},{110,112},{111,113}} | collective-permute-start | bytes 393224 | tf_op jit(solution)/shard_map/ppermute | solution.py:212
  176.8 9.2 %collective-permute-start.39 = (f32[32,1024]{1,0:T(8,128)}, f32[32,1024]{1,0:T(8,128)S(1)}, u32[]{:S(2)}, u32[]{:S(2)}) collective-permute-start(f32[32,1024]{1,0:T(8,128)} %get-tuple-element.225), channel_id=1, source_target_pairs={{14,16},{15,17},{46,48},{47,49},{78,80},{79,81},{110,112},{111,113}} | collective-permute-start | bytes 393224 | tf_op jit(solution)/shard_map/ppermute | solution.py:212
  178.9 8.5 %collective-permute-start.54 = (f32[32,1024]{1,0:T(8,128)}, f32[32,1024]{1,0:T(8,128)S(1)}, u32[]{:S(2)}, u32[]{:S(2)}) collective-permute-start(f32[32,1024]{1,0:T(8,128)} %get-tuple-element.253), channel_id=1, source_target_pairs={{14,16},{15,17},{46,48},{47,49},{78,80},{79,81},{110,112},{111,113}} | collective-permute-start | bytes 393224 | tf_op jit(solution)/shard_map/ppermute | solution.py:212
  181.8 23.6 %collective-permute-start.21 = (f32[32,1024]{1,0:T(8,128)}, f32[32,1024]{1,0:T(8,128)}, u32[]{:S(2)}, u32[]{:S(2)}) collective-permute-start(f32[32,1024]{1,0:T(8,128)} %get-tuple-element.188), channel_id=1, source_target_pairs={{14,16},{15,17},{46,48},{47,49},{78,80},{79,81},{110,112},{111,113}} | collective-permute-start | bytes 393224 | tf_op jit(solution)/shard_map/ppermute | solution.py:212
  185.3 33.3 %collective-permute-start.19 = (f32[32,1024]{1,0:T(8,128)}, f32[32,1024]{1,0:T(8,128)S(1)}, u32[]{:S(2)}, u32[]{:S(2)}) collective-permute-start(f32[32,1024]{1,0:T(8,128)} %get-tuple-element.183), channel_id=1, source_target_pairs={{16,18},{17,19},{48,50},{49,51},{80,82},{81,83},{112,114},{113,115}} | collective-permute-start | bytes 393224 | tf_op jit(solution)/shard_map/ppermute | solution.py:212
  186.7 46.1 %collective-permute-start.40 = (f32[32,1024]{1,0:T(8,128)}, f32[32,1024]{1,0:T(8,128)S(1)}, u32[]{:S(2)}, u32[]{:S(2)}) collective-permute-start(f32[32,1024]{1,0:T(8,128)} %get-tuple-element.227), channel_id=1, source_target_pairs={{16,18},{17,19},{48,50},{49,51},{80,82},{81,83},{112,114},{113,115}} | collective-permute-start | bytes 393224 | tf_op jit(solution)/shard_map/ppermute | solution.py:212
  188.1 55.6 %collective-permute-start.55 = (f32[32,1024]{1,0:T(8,128)}, f32[32,1024]{1,0:T(8,128)S(1)}, u32[]{:S(2)}, u32[]{:S(2)}) collective-permute-start(f32[32,1024]{1,0:T(8,128)} %get-tuple-element.255), channel_id=1, source_target_pairs={{16,18},{17,19},{48,50},{49,51},{80,82},{81,83},{112,114},{113,115}} | collective-permute-start | bytes 393224 | tf_op jit(solution)/shard_map/ppermute | solution.py:212
  207.0 46.9 %collective-permute-start.25 = (f32[32,1024]{1,0:T(8,128)}, f32[32,1024]{1,0:T(8,128)}, u32[]{:S(2)}, u32[]{:S(2)}) collective-permute-start(f32[32,1024]{1,0:T(8,128)} %get-tuple-element.198), channel_id=1, source_target_pairs={{16,18},{17,19},{48,50},{49,51},{80,82},{81,83},{112,114},{113,115}} | collective-permute-start | bytes 393224 | tf_op jit(solution)/shard_map/ppermute | solution.py:212
  208.3 10.4 %collective-permute-start.22 = (f32[8,128]{1,0:T(8,128)S(1)}, f32[8,128]{1,0:T(8,128)S(1)}, u32[]{:S(2)}, u32[]{:S(2)}) collective-permute-start(f32[8,128]{1,0:T(8,128)S(1)} %add.56), channel_id=1, source_target_pairs={{0,8},{1,9},{2,10},{3,11},{4,12},{5,13},{6,14},{7,15},{8,0},{9,1},... | collective-permute-start | bytes 12296 | tf_op jit(solution)/shard_map/ppermute | solution.py:207
  220.9 44.7 %collective-permute-start.23 = (f32[32,1024]{1,0:T(8,128)}, f32[32,1024]{1,0:T(8,128)}, u32[]{:S(2)}, u32[]{:S(2)}) collective-permute-start(f32[32,1024]{1,0:T(8,128)} %get-tuple-element.193), channel_id=1, source_target_pairs={{18,20},{19,21},{50,52},{51,53},{82,84},{83,85},{114,116},{115,117}} | collective-permute-start | bytes 393224 | tf_op jit(solution)/shard_map/ppermute | solution.py:212
  233.5 45.0 %collective-permute-start.41 = (f32[32,1024]{1,0:T(8,128)}, f32[32,1024]{1,0:T(8,128)}, u32[]{:S(2)}, u32[]{:S(2)}) collective-permute-start(f32[32,1024]{1,0:T(8,128)} %get-tuple-element.229), channel_id=1, source_target_pairs={{18,20},{19,21},{50,52},{51,53},{82,84},{83,85},{114,116},{115,117}} | collective-permute-start | bytes 393224 | tf_op jit(solution)/shard_map/ppermute | solution.py:212
  244.3 46.9 %collective-permute-start.56 = (f32[32,1024]{1,0:T(8,128)}, f32[32,1024]{1,0:T(8,128)S(1)}, u32[]{:S(2)}, u32[]{:S(2)}) collective-permute-start(f32[32,1024]{1,0:T(8,128)} %get-tuple-element.257), channel_id=1, source_target_pairs={{18,20},{19,21},{50,52},{51,53},{82,84},{83,85},{114,116},{115,117}} | collective-permute-start | bytes 393224 | tf_op jit(solution)/shard_map/ppermute | solution.py:212
  255.5 47.5 %collective-permute-start.26 = (f32[32,1024]{1,0:T(8,128)}, f32[32,1024]{1,0:T(8,128)}, u32[]{:S(2)}, u32[]{:S(2)}) collective-permute-start(f32[32,1024]{1,0:T(8,128)} %get-tuple-element.200), channel_id=1, source_target_pairs={{18,20},{19,21},{50,52},{51,53},{82,84},{83,85},{114,116},{115,117}} | collective-permute-start | bytes 393224 | tf_op jit(solution)/shard_map/ppermute | solution.py:212
  268.8 56.3 %collective-permute-start.24 = (f32[32,1024]{1,0:T(8,128)}, f32[32,1024]{1,0:T(8,128)S(1)}, u32[]{:S(2)}, u32[]{:S(2)}) collective-permute-start(f32[32,1024]{1,0:T(8,128)} %get-tuple-element.195), channel_id=1, source_target_pairs={{20,22},{21,23},{52,54},{53,55},{84,86},{85,87},{116,118},{117,119}} | collective-permute-start | bytes 393224 | tf_op jit(solution)/shard_map/ppermute | solution.py:212
  280.3 57.9 %collective-permute-start.42 = (f32[32,1024]{1,0:T(8,128)}, f32[32,1024]{1,0:T(8,128)S(1)}, u32[]{:S(2)}, u32[]{:S(2)}) collective-permute-start(f32[32,1024]{1,0:T(8,128)} %get-tuple-element.231), channel_id=1, source_target_pairs={{20,22},{21,23},{52,54},{53,55},{84,86},{85,87},{116,118},{117,119}} | collective-permute-start | bytes 393224 | tf_op jit(solution)/shard_map/ppermute | solution.py:212
  292.0 59.9 %collective-permute-start.57 = (f32[32,1024]{1,0:T(8,128)}, f32[32,1024]{1,0:T(8,128)S(1)}, u32[]{:S(2)}, u32[]{:S(2)}) collective-permute-start(f32[32,1024]{1,0:T(8,128)} %get-tuple-element.259), channel_id=1, source_target_pairs={{20,22},{21,23},{52,54},{53,55},{84,86},{85,87},{116,118},{117,119}} | collective-permute-start | bytes 393224 | tf_op jit(solution)/shard_map/ppermute | solution.py:212
  304.5 20.5 %collective-permute-start.27 = (f32[8,128]{1,0:T(8,128)S(1)}, f32[8,128]{1,0:T(8,128)S(1)}, u32[]{:S(2)}, u32[]{:S(2)}) collective-permute-start(f32[8,128]{1,0:T(8,128)S(1)} %add.57), channel_id=1, source_target_pairs={{0,16},{1,17},{2,18},{3,19},{4,20},{5,21},{6,22},{7,23},{8,24},{9,... | collective-permute-start | bytes 12296 | tf_op jit(solution)/shard_map/ppermute | solution.py:207
  314.9 49.0 %collective-permute-start.62 = (f32[32,1024]{1,0:T(8,128)}, f32[32,1024]{1,0:T(8,128)}, u32[]{:S(2)}, u32[]{:S(2)}) collective-permute-start(f32[32,1024]{1,0:T(8,128)} %copy-done.64), channel_id=1, source_target_pairs={{20,22},{21,23},{52,54},{53,55},{84,86},{85,87},{116,118},{117,119}} | collective-permute-start | bytes 393224 | tf_op jit(solution)/shard_map/ppermute | solution.py:212
  328.0 49.0 %collective-permute-start.28 = (f32[32,1024]{1,0:T(8,128)}, f32[32,1024]{1,0:T(8,128)S(1)}, u32[]{:S(2)}, u32[]{:S(2)}) collective-permute-start(f32[32,1024]{1,0:T(8,128)} %get-tuple-element.205), channel_id=1, source_target_pairs={{22,24},{23,25},{54,56},{55,57},{86,88},{87,89},{118,120},{119,121}} | collective-permute-start | bytes 393224 | tf_op jit(solution)/shard_map/ppermute | solution.py:212
  340.4 47.1 %collective-permute-start.43 = (f32[32,1024]{1,0:T(8,128)}, f32[32,1024]{1,0:T(8,128)}, u32[]{:S(2)}, u32[]{:S(2)}) collective-permute-start(f32[32,1024]{1,0:T(8,128)} %get-tuple-element.233), channel_id=1, source_target_pairs={{22,24},{23,25},{54,56},{55,57},{86,88},{87,89},{118,120},{119,121}} | collective-permute-start | bytes 393224 | tf_op jit(solution)/shard_map/ppermute | solution.py:212
  352.5 48.4 %collective-permute-start.58 = (f32[32,1024]{1,0:T(8,128)}, f32[32,1024]{1,0:T(8,128)}, u32[]{:S(2)}, u32[]{:S(2)}) collective-permute-start(f32[32,1024]{1,0:T(8,128)} %get-tuple-element.261), channel_id=1, source_target_pairs={{22,24},{23,25},{54,56},{55,57},{86,88},{87,89},{118,120},{119,121}} | collective-permute-start | bytes 393224 | tf_op jit(solution)/shard_map/ppermute | solution.py:212
  365.5 47.1 %collective-permute-start.63 = (f32[32,1024]{1,0:T(8,128)}, f32[32,1024]{1,0:T(8,128)}, u32[]{:S(2)}, u32[]{:S(2)}) collective-permute-start(f32[32,1024]{1,0:T(8,128)} %get-tuple-element.271), channel_id=1, source_target_pairs={{22,24},{23,25},{54,56},{55,57},{86,88},{87,89},{118,120},{119,121}} | collective-permute-start | bytes 393224 | tf_op jit(solution)/shard_map/ppermute | solution.py:212
  377.6 46.2 %collective-permute-start.29 = (f32[32,1024]{1,0:T(8,128)}, f32[32,1024]{1,0:T(8,128)S(1)}, u32[]{:S(2)}, u32[]{:S(2)}) collective-permute-start(f32[32,1024]{1,0:T(8,128)} %get-tuple-element.207), channel_id=1, source_target_pairs={{24,26},{25,27},{56,58},{57,59},{88,90},{89,91},{120,122},{121,123}} | collective-permute-start | bytes 393224 | tf_op jit(solution)/shard_map/ppermute | solution.py:212
  390.7 43.9 %collective-permute-start.44 = (f32[32,1024]{1,0:T(8,128)}, f32[32,1024]{1,0:T(8,128)}, u32[]{:S(2)}, u32[]{:S(2)}) collective-permute-start(f32[32,1024]{1,0:T(8,128)} %get-tuple-element.235), channel_id=1, source_target_pairs={{24,26},{25,27},{56,58},{57,59},{88,90},{89,91},{120,122},{121,123}} | collective-permute-start | bytes 393224 | tf_op jit(solution)/shard_map/ppermute | solution.py:212
  402.5 44.9 %collective-permute-start.59 = (f32[32,1024]{1,0:T(8,128)}, f32[32,1024]{1,0:T(8,128)}, u32[]{:S(2)}, u32[]{:S(2)}) collective-permute-start(f32[32,1024]{1,0:T(8,128)} %get-tuple-element.263), channel_id=1, source_target_pairs={{24,26},{25,27},{56,58},{57,59},{88,90},{89,91},{120,122},{121,123}} | collective-permute-start | bytes 393224 | tf_op jit(solution)/shard_map/ppermute | solution.py:212
  414.2 44.2 %collective-permute-start.64 = (f32[32,1024]{1,0:T(8,128)}, f32[32,1024]{1,0:T(8,128)S(1)}, u32[]{:S(2)}, u32[]{:S(2)}) collective-permute-start(f32[32,1024]{1,0:T(8,128)} %get-tuple-element.273), channel_id=1, source_target_pairs={{24,26},{25,27},{56,58},{57,59},{88,90},{89,91},{120,122},{121,123}} | collective-permute-start | bytes 393224 | tf_op jit(solution)/shard_map/ppermute | solution.py:212
  424.5 45.8 %collective-permute-start.30 = (f32[32,1024]{1,0:T(8,128)}, f32[32,1024]{1,0:T(8,128)}, u32[]{:S(2)}, u32[]{:S(2)}) collective-permute-start(f32[32,1024]{1,0:T(8,128)} %get-tuple-element.209), channel_id=1, source_target_pairs={{26,28},{27,29},{58,60},{59,61},{90,92},{91,93},{122,124},{123,125}} | collective-permute-start | bytes 393224 | tf_op jit(solution)/shard_map/ppermute | solution.py:212
  437.8 45.0 %collective-permute-start.45 = (f32[32,1024]{1,0:T(8,128)}, f32[32,1024]{1,0:T(8,128)S(1)}, u32[]{:S(2)}, u32[]{:S(2)}) collective-permute-start(f32[32,1024]{1,0:T(8,128)} %get-tuple-element.237), channel_id=1, source_target_pairs={{26,28},{27,29},{58,60},{59,61},{90,92},{91,93},{122,124},{123,125}} | collective-permute-start | bytes 393224 | tf_op jit(solution)/shard_map/ppermute | solution.py:212
  448.9 47.1 %collective-permute-start.60 = (f32[32,1024]{1,0:T(8,128)}, f32[32,1024]{1,0:T(8,128)S(1)}, u32[]{:S(2)}, u32[]{:S(2)}) collective-permute-start(f32[32,1024]{1,0:T(8,128)} %get-tuple-element.265), channel_id=1, source_target_pairs={{26,28},{27,29},{58,60},{59,61},{90,92},{91,93},{122,124},{123,125}} | collective-permute-start | bytes 393224 | tf_op jit(solution)/shard_map/ppermute | solution.py:212
  460.7 46.3 %collective-permute-start.65 = (f32[32,1024]{1,0:T(8,128)}, f32[32,1024]{1,0:T(8,128)S(1)}, u32[]{:S(2)}, u32[]{:S(2)}) collective-permute-start(f32[32,1024]{1,0:T(8,128)} %get-tuple-element.275), channel_id=1, source_target_pairs={{26,28},{27,29},{58,60},{59,61},{90,92},{91,93},{122,124},{123,125}} | collective-permute-start | bytes 393224 | tf_op jit(solution)/shard_map/ppermute | solution.py:212
  472.4 45.7 %collective-permute-start.31 = (f32[32,1024]{1,0:T(8,128)}, f32[32,1024]{1,0:T(8,128)}, u32[]{:S(2)}, u32[]{:S(2)}) collective-permute-start(f32[32,1024]{1,0:T(8,128)} %get-tuple-element.211), channel_id=1, source_target_pairs={{28,30},{29,31},{60,62},{61,63},{92,94},{93,95},{124,126},{125,127}} | collective-permute-start | bytes 393224 | tf_op jit(solution)/shard_map/ppermute | solution.py:212
  484.4 34.7 %collective-permute-start.46 = (f32[32,1024]{1,0:T(8,128)S(1)}, f32[32,1024]{1,0:T(8,128)S(1)}, u32[]{:S(2)}, u32[]{:S(2)}) collective-permute-start(f32[32,1024]{1,0:T(8,128)S(1)} %get-tuple-element.239), channel_id=1, source_target_pairs={{28,30},{29,31},{60,62},{61,63},{92,94},{93,95},{124,126},{125,127}} | collective-permute-start | bytes 393224 | tf_op jit(solution)/shard_map/ppermute | solution.py:212
  496.0 23.1 %collective-permute-start.61 = (f32[32,1024]{1,0:T(8,128)S(1)}, f32[32,1024]{1,0:T(8,128)S(1)}, u32[]{:S(2)}, u32[]{:S(2)}) collective-permute-start(f32[32,1024]{1,0:T(8,128)S(1)} %get-tuple-element.267), channel_id=1, source_target_pairs={{28,30},{29,31},{60,62},{61,63},{92,94},{93,95},{124,126},{125,127}} | collective-permute-start | bytes 393224 | tf_op jit(solution)/shard_map/ppermute | solution.py:212
  507.0 15.8 %collective-permute-start.66 = (f32[32,1024]{1,0:T(8,128)S(1)}, f32[32,1024]{1,0:T(8,128)S(1)}, u32[]{:S(2)}, u32[]{:S(2)}) collective-permute-start(f32[32,1024]{1,0:T(8,128)S(1)} %get-tuple-element.277), channel_id=1, source_target_pairs={{28,30},{29,31},{60,62},{61,63},{92,94},{93,95},{124,126},{125,127}} | collective-permute-start | bytes 393224 | tf_op jit(solution)/shard_map/ppermute | solution.py:212
  (79 other events, 277.3 us)
